TPU v7x, 256 devices: a whole 4x4x8 slice. The times are simulated.
256 devices in a mesh: ctx: 32 (over y, x, core), head: 8 (over z).
Axes of the slice: x: 4, y: 4, z: 8, core: 2. Of those that a mesh axis runs over, the one named last changes fastest.
Arguments:
- query_key: bfloat16 [16384, 1024], P('ctx', 'head'), may hold values from -6 to 6
- values: bfloat16 [16384, 4096], P('ctx', 'head'), may hold values from -6 to 6
- out_grad: bfloat16 [16384, 4096], P('ctx', 'head'), may hold values from -6 to 6
- out_weight: bfloat16 [4096, 4096], P('head'), may hold values from -0.09375 to 0.09375
- doc_lengths: int32 [128], replicated, may hold values from 1 to 2048, 16384 in all
Outputs:
- qk_grad: bfloat16 [16384, 1024], P('ctx', 'head')
- value_grad: bfloat16 [16384, 4096], P('ctx', 'head')
- proj_grad: float32 [4096, 4096], P('head', 'ctx')
Inputs may be any that keep to these rules, and one draw needn't show every extreme that they name: `doc_lengths`: the documents fill all 16384 positions in order; the longest has exactly 2048 tokens.
All inputs are finite; a program needn't handle non-finite values.
Results may differ from a plain program's by a relative error of at most 0.0068.
Values may be sent and summed in bfloat16 or wider, within the bound.
No kernel may reach another device: no remote copies, remote signals or barrier semaphores. Data moves between devices by JAX's collectives and lax.ppermute only.
A program may use at most 128 MiB of HBM per device.

v0:
```python
import functools
import math

import jax
import jax.numpy as jnp
import numpy as np
from jax import lax
from jax.experimental import pallas as pl
from jax.experimental.pallas import tpu as pltpu
from jax.sharding import PartitionSpec as P

HEAD = 128
QK = 16
HEADS = 4
TOK = 512
FEAT = 160
QUAD = 0.25 / math.sqrt(2.0)
bf16 = jnp.bfloat16
f32 = jnp.float32
MIB = 1024 * 1024
LIMIT = 20 * MIB


def feature_tables():
    pairs = [(a, b) for a in range(QK) for b in range(a, QK)]
    pick = np.zeros((FEAT, 2 * QK), np.float32)
    cols = np.zeros((FEAT, HEAD), np.float32)
    cols[0, :4] = (1.0, 1.0, 1.0, 1.0)
    for a in range(QK):
        pick[1 + a, a] = 1.0
        cols[1 + a, :4] = (0.0, 1.0, 0.5, 1.0)
    for n, (a, b) in enumerate(pairs):
        row = 1 + QK + n
        pick[row, a] = 1.0
        pick[row, QK + b] = 1.0
        cols[row, :4] = (0.0, 0.0, QUAD, 1.0 if a == b else 2.0)
    return pick, pick.T.copy(), cols


def place(i):
    return i // 8, (i // 2) % 4, i % 2


def index(y, x, k):
    return ((y % 4) * 4 + x % 4) * 2 + k


def along(dy, dx):
    return [(i, index(place(i)[0] + dy, place(i)[1] + dx, i % 2)) for i in range(32)]


def shift(k):
    return [(i, i + k) for i in range(32) if 0 <= i + k < 32]


def dot(a, b, ca, cb):
    return lax.dot_general(a, b, (((ca,), (cb,)), ((), ())), preferred_element_type=f32)


def call(body, outs, n_in, flops, nbytes, scalar=True, limit=LIMIT):
    specs = [pl.BlockSpec(memory_space=pltpu.VMEM)] * n_in
    if scalar:
        specs = [pl.BlockSpec(memory_space=pltpu.SMEM)] + specs
    return pl.pallas_call(
        body,
        out_shape=[jax.ShapeDtypeStruct(s, t) for s, t in outs],
        in_specs=specs,
        out_specs=[pl.BlockSpec(memory_space=pltpu.VMEM)] * len(outs),
        compiler_params=pltpu.CompilerParams(vmem_limit_bytes=limit),
        cost_estimate=pl.CostEstimate(flops=flops, bytes_accessed=nbytes, transcendentals=0),
    )


def lifted(pick, cols, x):
    a = dot(pick[:, :QK], x, 1, 0) + cols[:, 0:1]
    b = dot(pick[:, QK : 2 * QK], x, 1, 0) + cols[:, 1:2]
    return a, b, ((a * b) * cols[:, 2:3]).astype(bf16)


def split(x):
    high = x.astype(bf16)
    return high, (x - high.astype(f32)).astype(bf16)


def chain(pick_t, cols, g, a, b):
    scaled = g * cols[:, 2:3]
    out = jnp.zeros((QK, TOK), f32)
    for table, other in ((pick_t[:QK], b), (pick_t[QK : 2 * QK], a)):
        high, low = split(scaled * other)
        out = out + dot(table, high, 1, 0) + dot(table, low, 1, 0)
    return out


def put_norms(ref, norms):
    lane = lax.broadcasted_iota(jnp.int32, (FEAT, HEAD), 1)
    total = jnp.zeros((FEAT, HEAD), f32)
    for h in range(HEADS):
        high, low = split(norms[h])
        total = jnp.where(lane == h, high.astype(f32), total)
        total = jnp.where(lane == HEADS + h, low.astype(f32), total)
    ref[HEADS] = total.astype(bf16)


def norm_of(near, far, keep, h):
    def one(ref):
        part = ref[HEADS].astype(f32)
        return part[:, h : h + 1] + part[:, HEADS + h : HEADS + h + 1]

    return one(near) + keep * one(far)


def state_of(near, far, keep, h):
    return (near[h].astype(f32) + keep * far[h].astype(f32)).astype(bf16)


def local_state(ids, lens, qk, v, pick, cols, out, qkt, aux):
    off = ids[0].astype(f32)
    length = lens[...].astype(f32)
    later = lax.broadcasted_iota(jnp.int32, (128, 128), 1) < lax.broadcasted_iota(
        jnp.int32, (128, 128), 0
    )
    first = jnp.sum(jnp.where(later, length, 0.0), axis=1, keepdims=True) - off

    def doc_at(where_to):
        return jnp.max(jnp.where(first <= where_to, first, -1e9), axis=0, keepdims=True)

    start = doc_at(lax.broadcasted_iota(jnp.int32, (128, TOK), 1).astype(f32))
    last, prev, far = doc_at(TOK - 1.0), doc_at(-1.0), doc_at(3 * TOK - 1.0)
    ending = (start == last).astype(f32)
    aux[0:1] = start
    aux[1:2] = ending
    aux[2:3] = (start < 0.0).astype(f32)
    aux[3:4] = jnp.broadcast_to((last < 0.0).astype(f32), (1, TOK))
    aux[4:5] = jnp.broadcast_to((prev < -2.0 * TOK).astype(f32), (1, TOK))
    aux[5:6] = jnp.broadcast_to((far < 1.0 * TOK).astype(f32), (1, TOK))
    aux[6:8] = jnp.zeros((2, TOK), f32)
    qkt[...] = qk[...].astype(f32).T.astype(bf16)
    norms = []
    table, column = pick[...], cols[...]
    for h in range(HEADS):
        feat = lifted(table, column, qkt[32 * h + QK : 32 * h + 2 * QK])[2]
        feat = jnp.where(ending > 0.5, feat.astype(f32), 0.0)
        norms.append(jnp.sum(feat, axis=1, keepdims=True) * column[:, 3:4])
        state = dot(feat.astype(bf16), v[:, HEAD * h : HEAD * (h + 1)], 1, 0)
        out[h] = (state * column[:, 3:4]).astype(bf16)
    put_norms(out, norms)


def pair_sum(own, got, aux, out):
    keep = aux[3:4, 0:1]
    for h in range(HEADS):
        out[h] = (own[h].astype(f32) + keep * got[h].astype(f32)).astype(bf16)
    put_norms(out, [norm_of(own, got, keep, h) for h in range(HEADS)])


def scores_of(qkt, aux, h):
    q, k = qkt[32 * h : 32 * h + QK], qkt[32 * h + QK : 32 * h + 2 * QK]
    scores = dot(k, q, 0, 0) * 0.25
    row = lax.broadcasted_iota(jnp.int32, (TOK, TOK), 0)
    col = lax.broadcasted_iota(jnp.int32, (TOK, TOK), 1)
    visible = (row >= aux[0:1].astype(jnp.int32)) & (row <= col)
    return scores, visible, jnp.where(visible, 1.0 + scores + 0.5 * scores * scores, 0.0)


def attend(qkt, v, aux, pick, cols, near, far, att, quotient, dens):
    keep = aux[4:5, 0:1]
    carried = aux[2:3]
    table, column = pick[...], cols[...]
    for h in range(HEADS):
        rows = slice(HEAD * h, HEAD * (h + 1))
        weight = scores_of(qkt, aux, h)[2]
        feat = lifted(table, column, qkt[32 * h : 32 * h + QK])[2]
        norm = norm_of(near, far, keep, h)
        den = jnp.sum(weight, axis=0, keepdims=True)
        den = den + carried * jnp.sum(feat.astype(f32) * norm, axis=0, keepdims=True)
        num = dot(v[:, rows], weight.astype(bf16), 0, 0)
        num = num + carried * dot(state_of(near, far, keep, h), feat, 0, 0)
        y = num / den
        quotient[rows] = y
        att[rows] = y.astype(bf16)
        dens[h : h + 1] = den
    dens[HEADS:] = jnp.ones((8 - HEADS, TOK), f32)


def shard_of(ids, k):
    return lax.rem(ids[3] + k + 8, 8)


def partial_terms(count, ids, att, *refs):
    parts, (send, keep) = refs[: 2 * count], refs[2 * count :]
    first = ids[2] == 0
    half = TOK // 2
    for n in range(count):
        both = dot(att[:, :half], parts[2 * n][...], 1, 0)
        both = (both + dot(att[:, half:], parts[2 * n + 1][...], 1, 0)).astype(bf16)
        for j in range(2):
            even = both[:, 256 * j : 256 * j + HEAD]
            odd = both[:, 256 * j + HEAD : 256 * (j + 1)]
            send[2 * n + j] = jnp.where(first, odd, even)
            keep[2 * n + j] = jnp.where(first, even, odd)


def sum_cores(firsts, count, ids, *refs):
    outs, whole = refs[2 * count : -1], refs[-1]
    at = 0
    for group in range(count):
        keep, got = refs[group], refs[count + group]
        for n in range(keep.shape[0]):
            whole[at] = (keep[n].astype(f32) + got[n].astype(f32)).astype(bf16)
            at += 1
    for d in range(4):
        x = lax.rem(ids[5] + d, 4)
        for pair, k in enumerate(firsts):
            other = (lax.rem(shard_of(ids, k), 2) != x // 2).astype(jnp.int32)
            outs[d][pair] = whole[4 * pair + 2 * other + lax.rem(x, 2)]


def add_up(refs, *at):
    total = refs[0][at].astype(f32)
    for ref in refs[1:]:
        total = total + ref[at].astype(f32)
    return total


def sum_along_x(ids, *refs):
    ins, outs, whole = refs[:8], refs[8:12], refs[12]
    for group, places in enumerate(((0, 3), (1, 2))):
        for pair, slot in enumerate(places):
            whole[slot] = add_up(ins[4 * group : 4 * group + 4], pair)
    for d in range(4):
        shard = 2 * lax.rem(ids[4] + d, 4) + ids[5] // 2
        slot = lax.rem(shard - ids[3] + 8, 8) // 2
        outs[d][...] = whole[slot].astype(outs[d].dtype)


def sum_along_y(own, a, b, c, out):
    out[...] = add_up((own, a, b, c), Ellipsis)


def upstream(order, ids, w, *refs):
    parts, up = refs[:-1], refs[-1]
    half = TOK // 2
    for p in range(2):
        total = jnp.zeros((TOK, half), f32)
        for n, k in enumerate(order):
            at = pl.multiple_of(shard_of(ids, k) * TOK, TOK)
            total = total + dot(w[:, pl.ds(at, TOK)], parts[2 * n + p][...], 1, 1)
        up[:, half * p : half * (p + 1)] = total


def local_adjoint(up, quotient, dens, qkt, aux, pick, cols, ng, dg, out):
    carried = aux[2:3]
    table, column = pick[...], cols[...]
    norms = []
    for h in range(HEADS):
        rows = slice(HEAD * h, HEAD * (h + 1))
        inv = 1.0 / dens[h : h + 1]
        upstream = up[rows]
        den_grad = -jnp.sum(upstream * quotient[rows], axis=0, keepdims=True) * inv
        num_grad = (upstream * inv).astype(bf16)
        ng[rows] = num_grad
        dg[h : h + 1] = den_grad
        feat = lifted(table, column, qkt[32 * h : 32 * h + QK])[2]
        feat = feat.astype(f32) * carried
        norms.append(jnp.sum(feat * den_grad, axis=1, keepdims=True) * column[:, 3:4])
        out[h] = (dot(feat.astype(bf16), num_grad, 1, 1) * column[:, 3:4]).astype(bf16)
    dg[HEADS:] = jnp.zeros((8 - HEADS, TOK), f32)
    put_norms(out, norms)


def local_grads(ng, dg, qkt, v, aux, pick, pick_t, cols, near, far, qkg, vg):
    keep = aux[4:5, 0:1]
    carried = aux[2:3]
    table, column = pick[...], cols[...]
    for h in range(HEADS):
        rows = slice(HEAD * h, HEAD * (h + 1))
        q, k = qkt[32 * h : 32 * h + QK], qkt[32 * h + QK : 32 * h + 2 * QK]
        scores, visible, weight = scores_of(qkt, aux, h)
        num_grad, den_grad = ng[rows], dg[h : h + 1]
        mix = dot(v[:, rows], num_grad, 1, 0) + den_grad
        score_grad = jnp.where(visible, mix * (1.0 + scores), 0.0).astype(bf16)
        vg[:, rows] = dot(weight.astype(bf16), num_grad, 1, 1)
        a, b, _ = lifted(table, column, q)
        g = dot(state_of(near, far, keep, h), num_grad, 1, 0)
        g = carried * (g + norm_of(near, far, keep, h) * den_grad)
        qkg[32 * h : 32 * h + QK] = 0.25 * dot(k, score_grad, 1, 0) + chain(
            pick_t[...], column, g, a, b
        )
        qkg[32 * h + QK : 32 * h + 2 * QK] = 0.25 * dot(q, score_grad, 1, 1)


def finish(qkg, vg, qkt, v, aux, pick, pick_t, cols, near, far, qk_out, v_out, acc):
    keep = aux[5:6, 0:1]
    ending = aux[1:2]
    table, column = pick[...], cols[...]
    for h in range(HEADS):
        rows = slice(HEAD * h, HEAD * (h + 1))
        a, b, feat = lifted(table, column, qkt[32 * h + QK : 32 * h + 2 * QK])
        feat = (feat.astype(f32) * ending).astype(bf16)
        adjoint = state_of(near, far, keep, h)
        v_out[:, rows] = (vg[:, rows] + dot(feat, adjoint, 0, 0)).astype(bf16)
        g = dot(adjoint, v[:, rows], 1, 1) + norm_of(near, far, keep, h)
        acc[32 * h : 32 * h + QK] = qkg[32 * h : 32 * h + QK]
        acc[32 * h + QK : 32 * h + 2 * QK] = qkg[32 * h + QK : 32 * h + 2 * QK] + chain(
            pick_t[...], column, g * ending, a, b
        )
    qk_out[...] = acc[...].T.astype(bf16)


def on_device(query_key, values, out_grad, out_weight, doc_lengths):
    c = lax.axis_index("ctx").astype(jnp.int32)
    ids = jnp.stack([c * TOK, c // 2, c % 2, lax.axis_index("head").astype(jnp.int32), c // 8, (c // 2) % 4])
    np_pick, np_pick_t, np_cols = feature_tables()
    pick, pick_t, cols = jnp.asarray(np_pick, bf16), jnp.asarray(np_pick_t, bf16), jnp.asarray(np_cols)
    slab = ((HEADS + 1, FEAT, HEAD), bf16)

    half = TOK // 2
    own = lax.optimization_barrier([out_grad[:half], out_grad[half:]])
    query_key, own[0] = lax.optimization_barrier((query_key, own[0]))
    local, qkt, aux = call(
        local_state,
        [slab, ((128, TOK), bf16), ((8, TOK), f32)],
        5,
        2**27,
        2**21,
        limit=56 * MIB,
    )(ids, doc_lengths.reshape(1, 128), query_key, values, pick, cols)

    later, aux = lax.optimization_barrier((own[1], aux))
    own = [own[0], later]
    pieces = {0: own}
    ring = {d: [(i, (i + d) % 8) for i in range(8)] for d in (1, -1)}
    for step in range(1, 4):
        for d in (1, -1):
            before = pieces[-d * (step - 1)]
            pieces[-d * step] = [lax.ppermute(x, "head", ring[d]) for x in before]
    pieces[4] = [lax.ppermute(pieces[-3][0], "head", ring[1]), lax.ppermute(pieces[3][1], "head", ring[-1])]

    def exchange(mine, sign):
        got = lax.ppermute(mine, "ctx", shift(sign))
        pair = call(pair_sum, [slab], 3, 2**20, 2**20, False)(mine, got, aux)[0]
        return lax.ppermute(pair, "ctx", shift(sign)), lax.ppermute(pair, "ctx", shift(3 * sign))

    near, far = exchange(local, 1)
    att, quotient, dens = call(
        attend,
        [((TOK, TOK), bf16), ((TOK, TOK), f32), ((8, TOK), f32)],
        7,
        2**30,
        4 * 2**20,
        False,
    )(qkt, values, aux, pick, cols, near, far)

    send = lambda x, pairs: lax.ppermute(x, "ctx", pairs)

    def terms(shards):
        n = len(shards)
        block = ((2 * n, TOK, HEAD), bf16)
        out, keep = call(
            functools.partial(partial_terms, n), [block, block], 1 + 2 * n, n * 2**28, 2**20 * n
        )(ids, att, *[x for k in shards for x in pieces[k]])
        return keep, send(out, [(i, i ^ 1) for i in range(32)])

    def spread(firsts, found):
        count = len(found)
        parts = pl.pallas_call(
            functools.partial(sum_cores, firsts, count),
            out_shape=[jax.ShapeDtypeStruct((2, TOK, HEAD), bf16)] * 4,
            in_specs=[pl.BlockSpec(memory_space=pltpu.SMEM)]
            + [pl.BlockSpec(memory_space=pltpu.VMEM)] * (2 * count),
            out_specs=[pl.BlockSpec(memory_space=pltpu.VMEM)] * 4,
            scratch_shapes=[pltpu.VMEM((8, TOK, HEAD), bf16)],
            compiler_params=pltpu.CompilerParams(vmem_limit_bytes=LIMIT),
            cost_estimate=pl.CostEstimate(flops=2**20, bytes_accessed=2**21, transcendentals=0),
        )(ids, *[f[0] for f in found], *[f[1] for f in found])
        return [parts[0]] + [send(parts[d], along(0, d)) for d in (1, 3, 2)]

    steps = [(0, 1, -2, -1), (2, 3, 4, -3)]
    early = spread((0, -2), [terms((0, 1, -2, -1))])
    middle, late = terms((2, 3)), terms((4, -3))

    order = [k for shards in steps for k in shards]
    up = call(functools.partial(upstream, order), [((TOK, TOK), f32)], 17, 2**32, 9 * 2**20)(
        ids, out_weight, *[x for k in order for x in pieces[k]]
    )[0]

    ng, dg, adj_local = call(
        local_adjoint,
        [((TOK, TOK), bf16), ((8, TOK), f32), slab],
        7,
        2**28,
        4 * 2**20,
        False,
    )(up, quotient, dens, qkt, aux, pick, cols)
    adj_near, adj_far = exchange(adj_local, -1)
    kept, adj_local = lax.optimization_barrier((late[0], adj_local))
    rest = spread((2, 4), [middle, (kept, late[1])])
    qkg, vg = call(
        local_grads, [((128, TOK), f32), ((TOK, TOK), f32)], 10, 2**31, 4 * 2**20, False
    )(ng, dg, qkt, values, aux, pick, pick_t, cols, near, far)
    rest[0], vg = lax.optimization_barrier((rest[0], vg))
    sums = pl.pallas_call(
        sum_along_x,
        out_shape=[jax.ShapeDtypeStruct((TOK, HEAD), bf16 if d else f32) for d in range(4)],
        in_specs=[pl.BlockSpec(memory_space=pltpu.SMEM)]
        + [pl.BlockSpec(memory_space=pltpu.VMEM)] * 8,
        out_specs=[pl.BlockSpec(memory_space=pltpu.VMEM)] * 4,
        scratch_shapes=[pltpu.VMEM((4, TOK, HEAD), f32)],
        compiler_params=pltpu.CompilerParams(vmem_limit_bytes=LIMIT),
        cost_estimate=pl.CostEstimate(flops=2**20, bytes_accessed=2**21, transcendentals=0),
    )(ids, *early, *rest)
    across = [send(sums[d], along(d, 0)) for d in (1, 3, 2)]
    proj_grad = call(sum_along_y, [((TOK, HEAD), f32)], 4, 2**19, 2**20, False)(
        sums[0], *across
    )[0]
    qk_grad, value_grad = pl.pallas_call(
        finish,
        out_shape=[
            jax.ShapeDtypeStruct((TOK, 128), bf16),
            jax.ShapeDtypeStruct((TOK, TOK), bf16),
        ],
        in_specs=[pl.BlockSpec(memory_space=pltpu.VMEM)] * 10,
        out_specs=[pl.BlockSpec(memory_space=pltpu.VMEM)] * 2,
        scratch_shapes=[pltpu.VMEM((128, TOK), f32)],
        compiler_params=pltpu.CompilerParams(vmem_limit_bytes=LIMIT),
        cost_estimate=pl.CostEstimate(flops=2**29, bytes_accessed=4 * 2**20, transcendentals=0),
    )(qkg, vg, qkt, values, aux, pick, pick_t, cols, adj_near, adj_far)
    return (qk_grad, value_grad, proj_grad)


def solution(mesh):
    placed = (P("ctx", "head"), P("ctx", "head"), P("ctx", "head"), P("head", None), P())
    return jax.shard_map(
        on_device,
        mesh=mesh,
        in_specs=placed,
        out_specs=(P("ctx", "head"), P("ctx", "head"), P("head", "ctx")),
        check_vma=False,
    )
```

profile of v0, /device:TPU:14, one launch (start us, length us, event | category | flops | bytes accessed | tf_op | source)
XLA Modules:
  0.0 111.5 jit_solution(1432639474164081025)
XLA Ops:
  1.7 2.0 %collective-permute-start.2 = (bf16[256,512]{1,0:T(8,128)(2,1)S(1)}, bf16[256,512]{1,0:T(8,128)(2,1)S(1)}, u32[]{:S(2)}, u32[]{:S(2)}) collective-permute-start(bf16[256,512]{1,0:T(8,128)(2,1)S(1)} %get-tuple-element.44.refs_0_), channel_id=1, source_target_pairs={{0,1},{1,2},{2,3},{3,4},{4,5},{5,6},{6,7},{7,0},{8,9},{9,10},{10,1... | collective-permute-start | bytes 786440 | tf_op jit(solution)/shard_map/ppermute | solution.py:336
  4.3 3.1 %shard_map.103 = (bf16[5,160,128]{2,1,0:T(8,128)(2,1)}, bf16[128,512]{1,0:T(8,128)(2,1)}, f32[8,512]{1,0:T(8,128)}) custom-call(s32[6]{0:T(128)} %stack.27.ids, s32[1,128]{1,0:T(1,128)} %bitcast.7, bf16[512,128]{1,0:T(8,128)(2,1)} %qk, bf16[512,512]{1,0:T(8,128)(2,1)} %v.7, bf16[160,32]{1,0:T(8,128)(2,1)} %constant.63.clone.pick, f32[160,128]{1,0:T(8,128)} %constant.65.clone.cols), custom_call_target="tpu_custom_call" | custom-call | flops 134217728 | bytes 2097152 | tf_op jit(solution)/shard_map/pallas_call | solution.py:320
  7.4 4.0 %collective-permute-start.1 = (bf16[256,512]{1,0:T(8,128)(2,1)S(1)}, bf16[256,512]{1,0:T(8,128)(2,1)S(1)}, u32[]{:S(2)}, u32[]{:S(2)}) collective-permute-start(bf16[256,512]{1,0:T(8,128)(2,1)S(1)} %get-tuple-element.48.refs_1_), channel_id=1, source_target_pairs={{0,7},{1,0},{2,1},{3,2},{4,3},{5,4},{6,5},{7,6},{8,15},{9,8},{10,9... | collective-permute-start | bytes 786440 | tf_op jit(solution)/shard_map/ppermute | solution.py:336
  11.4 1.9 %collective-permute-start.14 = (bf16[5,160,128]{2,1,0:T(8,128)(2,1)}, bf16[5,160,128]{2,1,0:T(8,128)(2,1)S(1)}, u32[]{:S(2)}, u32[]{:S(2)}) collective-permute-start(bf16[5,160,128]{2,1,0:T(8,128)(2,1)} %get-tuple-element.51.own), channel_id=1, source_target_pairs={{0,8},{8,16},{16,24},{24,32},{32,40},{40,48},{48,56},{56,64},{64,7... | collective-permute-start | bytes 614408 | tf_op jit(solution)/shard_map/ppermute | solution.py:340
  13.3 2.0 %collective-permute-start = (bf16[256,512]{1,0:T(8,128)(2,1)S(1)}, bf16[256,512]{1,0:T(8,128)(2,1)S(1)}, u32[]{:S(2)}, u32[]{:S(2)}) collective-permute-start(bf16[256,512]{1,0:T(8,128)(2,1)S(1)} %get-tuple-element.44.refs_0_), channel_id=1, source_target_pairs={{0,7},{1,0},{2,1},{3,2},{4,3},{5,4},{6,5},{7,6},{8,15},{9,8},{10,9... | collective-permute-start | bytes 786440 | tf_op jit(solution)/shard_map/ppermute | solution.py:336
  17.0 3.7 %collective-permute-start.7 = (bf16[256,512]{1,0:T(8,128)(2,1)S(1)}, bf16[256,512]{1,0:T(8,128)(2,1)S(1)}, u32[]{:S(2)}, u32[]{:S(2)}) collective-permute-start(bf16[256,512]{1,0:T(8,128)(2,1)S(1)} %collective-permute-done.1.refs_3_), channel_id=1, source_target_pairs={{0,7},{1,0},{2,1},{3,2},{4,3},{5,4},{6,5},{7,6},{8,15},{9,8},{10,9... | collective-permute-start | bytes 786440 | tf_op jit(solution)/shard_map/ppermute | solution.py:336
  22.7 1.9 %collective-permute-start.16 = (bf16[5,160,128]{2,1,0:T(8,128)(2,1)S(1)}, bf16[5,160,128]{2,1,0:T(8,128)(2,1)S(1)}, u32[]{:S(2)}, u32[]{:S(2)}) collective-permute-start(bf16[5,160,128]{2,1,0:T(8,128)(2,1)S(1)} %shard_map.105), channel_id=1, source_target_pairs={{0,24},{8,32},{16,40},{24,48},{32,56},{40,64},{48,72},{56,80},{64,... | collective-permute-start | bytes 614408 | tf_op jit(solution)/shard_map/ppermute | solution.py:342
  24.6 4.4 %collective-permute-start.15 = (bf16[5,160,128]{2,1,0:T(8,128)(2,1)S(1)}, bf16[5,160,128]{2,1,0:T(8,128)(2,1)S(1)}, u32[]{:S(2)}, u32[]{:S(2)}) collective-permute-start(bf16[5,160,128]{2,1,0:T(8,128)(2,1)S(1)} %shard_map.105), channel_id=1, source_target_pairs={{0,8},{8,16},{16,24},{24,32},{32,40},{40,48},{48,56},{56,64},{64,7... | collective-permute-start | bytes 614408 | tf_op jit(solution)/shard_map/ppermute | solution.py:342
  32.2 2.4 %collective-permute-start.9 = (bf16[256,512]{1,0:T(8,128)(2,1)S(1)}, bf16[256,512]{1,0:T(8,128)(2,1)S(1)}, u32[]{:S(2)}, u32[]{:S(2)}) collective-permute-start(bf16[256,512]{1,0:T(8,128)(2,1)S(1)} %collective-permute-done.7.refs_9_.refs_1_), channel_id=1, source_target_pairs={{0,7},{1,0},{2,1},{3,2},{4,3},{5,4},{6,5},{7,6},{8,15},{9,8},{10,9... | collective-permute-start | bytes 786440 | tf_op jit(solution)/shard_map/ppermute | solution.py:336
  38.9 2.6 %shard_map.106 = (bf16[512,512]{1,0:T(8,128)(2,1)S(1)}, f32[512,512]{1,0:T(8,128)S(1)}, f32[8,512]{1,0:T(8,128)S(1)}) custom-call(bf16[128,512]{1,0:T(8,128)(2,1)S(1)} %copy-done.4, bf16[512,512]{1,0:T(8,128)(2,1)S(1)} %copy-done, f32[8,512]{1,0:T(8,128)S(1)} %copy-done.9, bf16[160,32]{1,0:T(8,128)(2,1)S(1)} %copy-done.6, f32[160,128]{1,0:T(8,128)S(1)} %copy-done.2, ...), custom_call_target="tpu_custom_call" | custom-call | flops 1073741824 | bytes 4194304 | tf_op jit(solution)/shard_map/pallas_call | solution.py:345
  41.6 2.2 %collective-permute-start.8 = (bf16[256,512]{1,0:T(8,128)(2,1)S(1)}, bf16[256,512]{1,0:T(8,128)(2,1)S(1)}, u32[]{:S(2)}, u32[]{:S(2)}) collective-permute-start(bf16[256,512]{1,0:T(8,128)(2,1)S(1)} %collective-permute-done.6.refs_8_.refs_0_), channel_id=1, source_target_pairs={{0,7},{1,0},{2,1},{3,2},{4,3},{5,4},{6,5},{7,6},{8,15},{9,8},{10,9... | collective-permute-start | bytes 786440 | tf_op jit(solution)/shard_map/ppermute | solution.py:336
  43.9 1.8 %collective-permute-done.10.refs_14_.refs_2_ = bf16[256,512]{1,0:T(8,128)(2,1)S(1)} collective-permute-done((bf16[256,512]{1,0:T(8,128)(2,1)S(1)}, bf16[256,512]{1,0:T(8,128)(2,1)S(1)}, u32[]{:S(2)}, u32[]{:S(2)}) %collective-permute-start.10) | collective-permute-done | bytes 262176 | tf_op jit(solution)/shard_map/ppermute | solution.py:336
  45.8 3.1 %collective-permute-start.12 = (bf16[256,512]{1,0:T(8,128)(2,1)S(1)}, bf16[256,512]{1,0:T(8,128)(2,1)S(1)}, u32[]{:S(2)}, u32[]{:S(2)}) collective-permute-start(bf16[256,512]{1,0:T(8,128)(2,1)S(1)} %collective-permute-done.9.refs_11_.refs_3_), channel_id=1, source_target_pairs={{0,7},{1,0},{2,1},{3,2},{4,3},{5,4},{6,5},{7,6},{8,15},{9,8},{10,9... | collective-permute-start | bytes 786440 | tf_op jit(solution)/shard_map/ppermute | solution.py:337
  48.9 1.8 %shard_map.114 = (bf16[8,512,128]{2,1,0:T(8,128)(2,1)S(1)}, bf16[8,512,128]{2,1,0:T(8,128)(2,1)S(1)}) custom-call(s32[6]{0:T(128)S(1)} %copy-done.13, bf16[512,512]{1,0:T(8,128)(2,1)S(1)} %get-tuple-element.57.att, bf16[256,512]{1,0:T(8,128)(2,1)S(1)} %get-tuple-element.44.refs_0_, bf16[256,512]{1,0:T(8,128)(2,1)S(1)} %get-tuple-element.48.refs_1_, ...), custom_call_target="tpu_custom_call" | custom-call | flops 1073741824 | bytes 4194304 | tf_op jit(solution)/shard_map/pallas_call | solution.py:359
  52.7 1.6 %collective-permute-done.13.refs_15_.refs_3_ = bf16[256,512]{1,0:T(8,128)(2,1)S(1)} collective-permute-done((bf16[256,512]{1,0:T(8,128)(2,1)S(1)}, bf16[256,512]{1,0:T(8,128)(2,1)S(1)}, u32[]{:S(2)}, u32[]{:S(2)}) %collective-permute-start.13) | collective-permute-done | bytes 262176 | tf_op jit(solution)/shard_map/ppermute | solution.py:336
  54.2 2.8 %collective-permute-done.11.refs_12_.refs_0_ = bf16[256,512]{1,0:T(8,128)(2,1)S(1)} collective-permute-done((bf16[256,512]{1,0:T(8,128)(2,1)S(1)}, bf16[256,512]{1,0:T(8,128)(2,1)S(1)}, u32[]{:S(2)}, u32[]{:S(2)}) %collective-permute-start.11) | collective-permute-done | bytes 262176 | tf_op jit(solution)/shard_map/ppermute | solution.py:337
  58.5 2.9 %shard_map.104.up = f32[512,512]{1,0:T(8,128)S(1)} custom-call(s32[6]{0:T(128)S(1)} %copy-done.13, bf16[512,4096]{1,0:T(8,128)(2,1)S(1)} %copy-done.14, bf16[256,512]{1,0:T(8,128)(2,1)S(1)} %get-tuple-element.44.refs_0_, bf16[256,512]{1,0:T(8,128)(2,1)S(1)} %get-tuple-element.48.refs_1_, bf16[256,512]{1,0:T(8,128)(2,1)S(1)} %collective-permute-done.refs_2_, ...), custom_call_target="tpu_custom_call" | custom-call | flops 4294967296 | bytes 9437184 | tf_op jit(solution)/shard_map/pallas_call | solution.py:383
  63.6 1.9 %collective-permute-start.26 = (bf16[2,512,128]{2,1,0:T(8,128)(2,1)S(1)}, bf16[2,512,128]{2,1,0:T(8,128)(2,1)S(1)}, u32[]{:S(2)}, u32[]{:S(2)}) collective-permute-start(bf16[2,512,128]{2,1,0:T(8,128)(2,1)S(1)} %get-tuple-element.76), channel_id=1, source_target_pairs={{0,16},{8,24},{16,32},{24,40},{32,48},{40,56},{48,0},{56,8},{64,80... | collective-permute-start | bytes 786440 | tf_op jit(solution)/shard_map/ppermute | solution.py:354
  65.5 1.9 %collective-permute-start.19 = (bf16[5,160,128]{2,1,0:T(8,128)(2,1)S(1)}, bf16[5,160,128]{2,1,0:T(8,128)(2,1)S(1)}, u32[]{:S(2)}, u32[]{:S(2)}) collective-permute-start(bf16[5,160,128]{2,1,0:T(8,128)(2,1)S(1)} %get-tuple-element.60.own), channel_id=1, source_target_pairs={{8,0},{16,8},{24,16},{32,24},{40,32},{48,40},{56,48},{64,56},{72,6... | collective-permute-start | bytes 614408 | tf_op jit(solution)/shard_map/ppermute | solution.py:340
  68.0 2.7 %collective-permute-start.28 = (bf16[2,512,128]{2,1,0:T(8,128)(2,1)S(1)}, bf16[2,512,128]{2,1,0:T(8,128)(2,1)S(1)}, u32[]{:S(2)}, u32[]{:S(2)}) collective-permute-start(bf16[2,512,128]{2,1,0:T(8,128)(2,1)S(1)} %get-tuple-element.78), channel_id=1, source_target_pairs={{0,32},{8,40},{16,48},{24,56},{32,0},{40,8},{48,16},{56,24},{64,96... | collective-permute-start | bytes 786440 | tf_op jit(solution)/shard_map/ppermute | solution.py:354
  73.9 2.8 %collective-permute-done.26.refs_5_ = bf16[2,512,128]{2,1,0:T(8,128)(2,1)S(1)} collective-permute-done((bf16[2,512,128]{2,1,0:T(8,128)(2,1)S(1)}, bf16[2,512,128]{2,1,0:T(8,128)(2,1)S(1)}, u32[]{:S(2)}, u32[]{:S(2)}) %collective-permute-start.26) | collective-permute-done | bytes 262176 | tf_op jit(solution)/shard_map/ppermute | solution.py:354
  77.1 5.1 %collective-permute-done.27.refs_6_ = bf16[2,512,128]{2,1,0:T(8,128)(2,1)S(1)} collective-permute-done((bf16[2,512,128]{2,1,0:T(8,128)(2,1)S(1)}, bf16[2,512,128]{2,1,0:T(8,128)(2,1)S(1)}, u32[]{:S(2)}, u32[]{:S(2)}) %collective-permute-start.27) | collective-permute-done | bytes 262176 | tf_op jit(solution)/shard_map/ppermute | solution.py:354
  82.3 1.9 %collective-permute-start.21 = (bf16[5,160,128]{2,1,0:T(8,128)(2,1)S(1)}, bf16[5,160,128]{2,1,0:T(8,128)(2,1)S(1)}, u32[]{:S(2)}, u32[]{:S(2)}) collective-permute-start(bf16[5,160,128]{2,1,0:T(8,128)(2,1)S(1)} %shard_map.112), channel_id=1, source_target_pairs={{24,0},{32,8},{40,16},{48,24},{56,32},{64,40},{72,48},{80,56},{88,... | collective-permute-start | bytes 614408 | tf_op jit(solution)/shard_map/ppermute | solution.py:342
  84.2 1.8 %collective-permute-done.28.refs_7_ = bf16[2,512,128]{2,1,0:T(8,128)(2,1)S(1)} collective-permute-done((bf16[2,512,128]{2,1,0:T(8,128)(2,1)S(1)}, bf16[2,512,128]{2,1,0:T(8,128)(2,1)S(1)}, u32[]{:S(2)}, u32[]{:S(2)}) %collective-permute-start.28) | collective-permute-done | bytes 262176 | tf_op jit(solution)/shard_map/ppermute | solution.py:354
  86.0 1.9 %collective-permute-start.20 = (bf16[5,160,128]{2,1,0:T(8,128)(2,1)S(1)}, bf16[5,160,128]{2,1,0:T(8,128)(2,1)S(1)}, u32[]{:S(2)}, u32[]{:S(2)}) collective-permute-start(bf16[5,160,128]{2,1,0:T(8,128)(2,1)S(1)} %shard_map.112), channel_id=1, source_target_pairs={{8,0},{16,8},{24,16},{32,24},{40,32},{48,40},{56,48},{64,56},{72,6... | collective-permute-start | bytes 614408 | tf_op jit(solution)/shard_map/ppermute | solution.py:342
  87.9 3.9 %shard_map.108 = (f32[128,512]{1,0:T(8,128)S(1)}, f32[512,512]{1,0:T(8,128)S(1)}) custom-call(bf16[512,512]{1,0:T(8,128)(2,1)S(1)} %get-tuple-element.54.ng, f32[8,512]{1,0:T(8,128)S(1)} %get-tuple-element.55.dg, bf16[128,512]{1,0:T(8,128)(2,1)S(1)} %copy-done.5, bf16[512,512]{1,0:T(8,128)(2,1)S(1)} %copy-done.1, f32[8,512]{1,0:T(8,128)S(1)} %copy-done.10, ...), custom_call_target="tpu_custom_call" | custom-call | flops 2147483648 | bytes 4194304 | tf_op jit(solution)/shard_map/pallas_call | solution.py:398
  91.9 1.6 %collective-permute-done.24.refs_2_ = bf16[2,512,128]{2,1,0:T(8,128)(2,1)S(1)} collective-permute-done((bf16[2,512,128]{2,1,0:T(8,128)(2,1)S(1)}, bf16[2,512,128]{2,1,0:T(8,128)(2,1)S(1)}, u32[]{:S(2)}, u32[]{:S(2)}) %collective-permute-start.24) | collective-permute-done | bytes 262176 | tf_op jit(solution)/shard_map/ppermute | solution.py:354
  93.5 3.4 %collective-permute-done.25.refs_3_ = bf16[2,512,128]{2,1,0:T(8,128)(2,1)S(1)} collective-permute-done((bf16[2,512,128]{2,1,0:T(8,128)(2,1)S(1)}, bf16[2,512,128]{2,1,0:T(8,128)(2,1)S(1)}, u32[]{:S(2)}, u32[]{:S(2)}) %collective-permute-start.25) | collective-permute-done | bytes 262176 | tf_op jit(solution)/shard_map/ppermute | solution.py:354
  97.8 5.1 %collective-permute-start.29 = (bf16[512,128]{1,0:T(8,128)(2,1)S(1)}, bf16[512,128]{1,0:T(8,128)(2,1)S(1)}, u32[]{:S(2)}, u32[]{:S(2)}) collective-permute-start(bf16[512,128]{1,0:T(8,128)(2,1)S(1)} %get-tuple-element.80), channel_id=1, source_target_pairs={{0,64},{8,72},{16,80},{24,88},{32,96},{40,104},{48,112},{56,120},{... | collective-permute-start | bytes 393224 | tf_op jit(solution)/shard_map/ppermute | solution.py:354
  102.9 1.6 %collective-permute-start.31 = (bf16[512,128]{1,0:T(8,128)(2,1)S(1)}, bf16[512,128]{1,0:T(8,128)(2,1)S(1)}, u32[]{:S(2)}, u32[]{:S(2)}) collective-permute-start(bf16[512,128]{1,0:T(8,128)(2,1)S(1)} %get-tuple-element.82), channel_id=1, source_target_pairs={{0,128},{8,136},{16,144},{24,152},{32,160},{40,168},{48,176},{56,1... | collective-permute-start | bytes 393224 | tf_op jit(solution)/shard_map/ppermute | solution.py:354
  104.4 3.2 %shard_map.113 = (bf16[512,128]{1,0:T(8,128)(2,1)}, bf16[512,512]{1,0:T(8,128)(2,1)}) custom-call(f32[128,512]{1,0:T(8,128)S(1)} %get-tuple-element.56.qkg, f32[512,512]{1,0:T(8,128)S(1)} %get-tuple-element.66.vg, bf16[128,512]{1,0:T(8,128)(2,1)S(1)} %copy-done.5, bf16[512,512]{1,0:T(8,128)(2,1)S(1)} %copy-done.1, f32[8,512]{1,0:T(8,128)S(1)} %copy-done.10, ...), custom_call_target="tpu_custom_call" | custom-call | flops 536870912 | bytes 4194304 | tf_op jit(solution)/shard_map/pallas_call | solution.py:416
  108.8 1.9 %collective-permute-done.31.c = bf16[512,128]{1,0:T(8,128)(2,1)S(1)} collective-permute-done((bf16[512,128]{1,0:T(8,128)(2,1)S(1)}, bf16[512,128]{1,0:T(8,128)(2,1)S(1)}, u32[]{:S(2)}, u32[]{:S(2)}) %collective-permute-start.31) | collective-permute-done | bytes 131104 | tf_op jit(solution)/shard_map/ppermute | solution.py:354
  (79 shorter events, 25.3 us)
Async XLA Ops:
  1.7 13.7 %collective-permute-start.2 = (bf16[256,512]{1,0:T(8,128)(2,1)S(1)}, bf16[256,512]{1,0:T(8,128)(2,1)S(1)}, u32[]{:S(2)}, u32[]{:S(2)}) collective-permute-start(bf16[256,512]{1,0:T(8,128)(2,1)S(1)} %get-tuple-element.44.refs_0_), channel_id=1, source_target_pairs={{0,1},{1,2},{2,3},{3,4},{4,5},{5,6},{6,7},{7,0},{8,9},{9,10},{10,1... | collective-permute-start | bytes 786440 | tf_op jit(solution)/shard_map/ppermute | solution.py:336
  7.4 9.6 %collective-permute-start.1 = (bf16[256,512]{1,0:T(8,128)(2,1)S(1)}, bf16[256,512]{1,0:T(8,128)(2,1)S(1)}, u32[]{:S(2)}, u32[]{:S(2)}) collective-permute-start(bf16[256,512]{1,0:T(8,128)(2,1)S(1)} %get-tuple-element.48.refs_1_), channel_id=1, source_target_pairs={{0,7},{1,0},{2,1},{3,2},{4,3},{5,4},{6,5},{7,6},{8,15},{9,8},{10,9... | collective-permute-start | bytes 786440 | tf_op jit(solution)/shard_map/ppermute | solution.py:336
  11.4 9.3 %collective-permute-start.14 = (bf16[5,160,128]{2,1,0:T(8,128)(2,1)}, bf16[5,160,128]{2,1,0:T(8,128)(2,1)S(1)}, u32[]{:S(2)}, u32[]{:S(2)}) collective-permute-start(bf16[5,160,128]{2,1,0:T(8,128)(2,1)} %get-tuple-element.51.own), channel_id=1, source_target_pairs={{0,8},{8,16},{16,24},{24,32},{32,40},{40,48},{48,56},{56,64},{64,7... | collective-permute-start | bytes 614408 | tf_op jit(solution)/shard_map/ppermute | solution.py:340
  13.3 11.3 %collective-permute-start = (bf16[256,512]{1,0:T(8,128)(2,1)S(1)}, bf16[256,512]{1,0:T(8,128)(2,1)S(1)}, u32[]{:S(2)}, u32[]{:S(2)}) collective-permute-start(bf16[256,512]{1,0:T(8,128)(2,1)S(1)} %get-tuple-element.44.refs_0_), channel_id=1, source_target_pairs={{0,7},{1,0},{2,1},{3,2},{4,3},{5,4},{6,5},{7,6},{8,15},{9,8},{10,9... | collective-permute-start | bytes 786440 | tf_op jit(solution)/shard_map/ppermute | solution.py:336
  15.4 13.7 %collective-permute-start.4 = (bf16[256,512]{1,0:T(8,128)(2,1)S(1)}, bf16[256,512]{1,0:T(8,128)(2,1)S(1)}, u32[]{:S(2)}, u32[]{:S(2)}) collective-permute-start(bf16[256,512]{1,0:T(8,128)(2,1)S(1)} %get-tuple-element.48.refs_1_), channel_id=1, source_target_pairs={{0,1},{1,2},{2,3},{3,4},{4,5},{5,6},{6,7},{7,0},{8,9},{9,10},{10,1... | collective-permute-start | bytes 786440 | tf_op jit(solution)/shard_map/ppermute | solution.py:336
  15.4 15.9 %collective-permute-start.3 = (bf16[256,512]{1,0:T(8,128)(2,1)S(1)}, bf16[256,512]{1,0:T(8,128)(2,1)S(1)}, u32[]{:S(2)}, u32[]{:S(2)}) collective-permute-start(bf16[256,512]{1,0:T(8,128)(2,1)S(1)} %collective-permute-done.2.refs_6_), channel_id=1, source_target_pairs={{0,1},{1,2},{2,3},{3,4},{4,5},{5,6},{6,7},{7,0},{8,9},{9,10},{10,1... | collective-permute-start | bytes 786440 | tf_op jit(solution)/shard_map/ppermute | solution.py:336
  17.0 15.2 %collective-permute-start.7 = (bf16[256,512]{1,0:T(8,128)(2,1)S(1)}, bf16[256,512]{1,0:T(8,128)(2,1)S(1)}, u32[]{:S(2)}, u32[]{:S(2)}) collective-permute-start(bf16[256,512]{1,0:T(8,128)(2,1)S(1)} %collective-permute-done.1.refs_3_), channel_id=1, source_target_pairs={{0,7},{1,0},{2,1},{3,2},{4,3},{5,4},{6,5},{7,6},{8,15},{9,8},{10,9... | collective-permute-start | bytes 786440 | tf_op jit(solution)/shard_map/ppermute | solution.py:336
  22.7 8.6 %collective-permute-start.16 = (bf16[5,160,128]{2,1,0:T(8,128)(2,1)S(1)}, bf16[5,160,128]{2,1,0:T(8,128)(2,1)S(1)}, u32[]{:S(2)}, u32[]{:S(2)}) collective-permute-start(bf16[5,160,128]{2,1,0:T(8,128)(2,1)S(1)} %shard_map.105), channel_id=1, source_target_pairs={{0,24},{8,32},{16,40},{24,48},{32,56},{40,64},{48,72},{56,80},{64,... | collective-permute-start | bytes 614408 | tf_op jit(solution)/shard_map/ppermute | solution.py:342
  24.6 10.0 %collective-permute-start.15 = (bf16[5,160,128]{2,1,0:T(8,128)(2,1)S(1)}, bf16[5,160,128]{2,1,0:T(8,128)(2,1)S(1)}, u32[]{:S(2)}, u32[]{:S(2)}) collective-permute-start(bf16[5,160,128]{2,1,0:T(8,128)(2,1)S(1)} %shard_map.105), channel_id=1, source_target_pairs={{0,8},{8,16},{16,24},{24,32},{32,40},{40,48},{48,56},{56,64},{64,7... | collective-permute-start | bytes 614408 | tf_op jit(solution)/shard_map/ppermute | solution.py:342
  29.1 12.5 %collective-permute-start.6 = (bf16[256,512]{1,0:T(8,128)(2,1)S(1)}, bf16[256,512]{1,0:T(8,128)(2,1)S(1)}, u32[]{:S(2)}, u32[]{:S(2)}) collective-permute-start(bf16[256,512]{1,0:T(8,128)(2,1)S(1)} %collective-permute-done.refs_2_), channel_id=1, source_target_pairs={{0,7},{1,0},{2,1},{3,2},{4,3},{5,4},{6,5},{7,6},{8,15},{9,8},{10,9... | collective-permute-start | bytes 786440 | tf_op jit(solution)/shard_map/ppermute | solution.py:336
  31.3 12.5 %collective-permute-start.5 = (bf16[256,512]{1,0:T(8,128)(2,1)S(1)}, bf16[256,512]{1,0:T(8,128)(2,1)S(1)}, u32[]{:S(2)}, u32[]{:S(2)}) collective-permute-start(bf16[256,512]{1,0:T(8,128)(2,1)S(1)} %collective-permute-done.4.refs_7_), channel_id=1, source_target_pairs={{0,1},{1,2},{2,3},{3,4},{4,5},{5,6},{6,7},{7,0},{8,9},{9,10},{10,1... | collective-permute-start | bytes 786440 | tf_op jit(solution)/shard_map/ppermute | solution.py:336
  31.3 14.4 %collective-permute-start.10 = (bf16[256,512]{1,0:T(8,128)(2,1)S(1)}, bf16[256,512]{1,0:T(8,128)(2,1)S(1)}, u32[]{:S(2)}, u32[]{:S(2)}) collective-permute-start(bf16[256,512]{1,0:T(8,128)(2,1)S(1)} %collective-permute-done.3.refs_4_), channel_id=1, source_target_pairs={{0,1},{1,2},{2,3},{3,4},{4,5},{5,6},{6,7},{7,0},{8,9},{9,10},{10,1... | collective-permute-start | bytes 786440 | tf_op jit(solution)/shard_map/ppermute | solution.py:336
  32.2 13.6 %collective-permute-start.9 = (bf16[256,512]{1,0:T(8,128)(2,1)S(1)}, bf16[256,512]{1,0:T(8,128)(2,1)S(1)}, u32[]{:S(2)}, u32[]{:S(2)}) collective-permute-start(bf16[256,512]{1,0:T(8,128)(2,1)S(1)} %collective-permute-done.7.refs_9_.refs_1_), channel_id=1, source_target_pairs={{0,7},{1,0},{2,1},{3,2},{4,3},{5,4},{6,5},{7,6},{8,15},{9,8},{10,9... | collective-permute-start | bytes 786440 | tf_op jit(solution)/shard_map/ppermute | solution.py:336
  41.6 9.5 %collective-permute-start.8 = (bf16[256,512]{1,0:T(8,128)(2,1)S(1)}, bf16[256,512]{1,0:T(8,128)(2,1)S(1)}, u32[]{:S(2)}, u32[]{:S(2)}) collective-permute-start(bf16[256,512]{1,0:T(8,128)(2,1)S(1)} %collective-permute-done.6.refs_8_.refs_0_), channel_id=1, source_target_pairs={{0,7},{1,0},{2,1},{3,2},{4,3},{5,4},{6,5},{7,6},{8,15},{9,8},{10,9... | collective-permute-start | bytes 786440 | tf_op jit(solution)/shard_map/ppermute | solution.py:336
  43.8 10.5 %collective-permute-start.13 = (bf16[256,512]{1,0:T(8,128)(2,1)S(1)}, bf16[256,512]{1,0:T(8,128)(2,1)S(1)}, u32[]{:S(2)}, u32[]{:S(2)}) collective-permute-start(bf16[256,512]{1,0:T(8,128)(2,1)S(1)} %collective-permute-done.5.refs_5_), channel_id=1, source_target_pairs={{0,1},{1,2},{2,3},{3,4},{4,5},{5,6},{6,7},{7,0},{8,9},{9,10},{10,1... | collective-permute-start | bytes 786440 | tf_op jit(solution)/shard_map/ppermute | solution.py:336
  45.7 11.4 %collective-permute-start.11 = (bf16[256,512]{1,0:T(8,128)(2,1)S(1)}, bf16[256,512]{1,0:T(8,128)(2,1)S(1)}, u32[]{:S(2)}, u32[]{:S(2)}) collective-permute-start(bf16[256,512]{1,0:T(8,128)(2,1)S(1)} %collective-permute-done.10.refs_14_.refs_2_), channel_id=1, source_target_pairs={{0,1},{1,2},{2,3},{3,4},{4,5},{5,6},{6,7},{7,0},{8,9},{9,10},{10,1... | collective-permute-start | bytes 786440 | tf_op jit(solution)/shard_map/ppermute | solution.py:337
  45.8 11.3 %collective-permute-start.12 = (bf16[256,512]{1,0:T(8,128)(2,1)S(1)}, bf16[256,512]{1,0:T(8,128)(2,1)S(1)}, u32[]{:S(2)}, u32[]{:S(2)}) collective-permute-start(bf16[256,512]{1,0:T(8,128)(2,1)S(1)} %collective-permute-done.9.refs_11_.refs_3_), channel_id=1, source_target_pairs={{0,7},{1,0},{2,1},{3,2},{4,3},{5,4},{6,5},{7,6},{8,15},{9,8},{10,9... | collective-permute-start | bytes 786440 | tf_op jit(solution)/shard_map/ppermute | solution.py:337
  50.7 19.9 %collective-permute-start.22 = (bf16[8,512,128]{2,1,0:T(8,128)(2,1)S(1)}, bf16[8,512,128]{2,1,0:T(8,128)(2,1)S(1)}, u32[]{:S(2)}, u32[]{:S(2)}) collective-permute-start(bf16[8,512,128]{2,1,0:T(8,128)(2,1)S(1)} %get-tuple-element.70), channel_id=1, source_target_pairs={{0,8},{8,0},{16,24},{24,16},{32,40},{40,32},{48,56},{56,48},{64,72... | collective-permute-start | bytes 3145736 | tf_op jit(solution)/shard_map/ppermute | solution.py:354
  52.3 10.3 %collective-permute-start.17 = (bf16[4,512,128]{2,1,0:T(8,128)(2,1)S(1)}, bf16[4,512,128]{2,1,0:T(8,128)(2,1)S(1)}, u32[]{:S(2)}, u32[]{:S(2)}) collective-permute-start(bf16[4,512,128]{2,1,0:T(8,128)(2,1)S(1)} %get-tuple-element.62), channel_id=1, source_target_pairs={{0,8},{8,0},{16,24},{24,16},{32,40},{40,32},{48,56},{56,48},{64,72... | collective-permute-start | bytes 1572872 | tf_op jit(solution)/shard_map/ppermute | solution.py:354
  58.4 4.2 %collective-permute-start.18 = (bf16[4,512,128]{2,1,0:T(8,128)(2,1)S(1)}, bf16[4,512,128]{2,1,0:T(8,128)(2,1)S(1)}, u32[]{:S(2)}, u32[]{:S(2)}) collective-permute-start(bf16[4,512,128]{2,1,0:T(8,128)(2,1)S(1)} %get-tuple-element.63), channel_id=1, source_target_pairs={{0,8},{8,0},{16,24},{24,16},{32,40},{40,32},{48,56},{56,48},{64,72... | collective-permute-start | bytes 1572872 | tf_op jit(solution)/shard_map/ppermute | solution.py:354
  63.6 13.1 %collective-permute-start.26 = (bf16[2,512,128]{2,1,0:T(8,128)(2,1)S(1)}, bf16[2,512,128]{2,1,0:T(8,128)(2,1)S(1)}, u32[]{:S(2)}, u32[]{:S(2)}) collective-permute-start(bf16[2,512,128]{2,1,0:T(8,128)(2,1)S(1)} %get-tuple-element.76), channel_id=1, source_target_pairs={{0,16},{8,24},{16,32},{24,40},{32,48},{40,56},{48,0},{56,8},{64,80... | collective-permute-start | bytes 786440 | tf_op jit(solution)/shard_map/ppermute | solution.py:354
  65.5 7.4 %collective-permute-start.19 = (bf16[5,160,128]{2,1,0:T(8,128)(2,1)S(1)}, bf16[5,160,128]{2,1,0:T(8,128)(2,1)S(1)}, u32[]{:S(2)}, u32[]{:S(2)}) collective-permute-start(bf16[5,160,128]{2,1,0:T(8,128)(2,1)S(1)} %get-tuple-element.60.own), channel_id=1, source_target_pairs={{8,0},{16,8},{24,16},{32,24},{40,32},{48,40},{56,48},{64,56},{72,6... | collective-permute-start | bytes 614408 | tf_op jit(solution)/shard_map/ppermute | solution.py:340
  67.4 14.9 %collective-permute-start.27 = (bf16[2,512,128]{2,1,0:T(8,128)(2,1)S(1)}, bf16[2,512,128]{2,1,0:T(8,128)(2,1)S(1)}, u32[]{:S(2)}, u32[]{:S(2)}) collective-permute-start(bf16[2,512,128]{2,1,0:T(8,128)(2,1)S(1)} %get-tuple-element.77), channel_id=1, source_target_pairs={{0,48},{8,56},{16,0},{24,8},{32,16},{40,24},{48,32},{56,40},{64,11... | collective-permute-start | bytes 786440 | tf_op jit(solution)/shard_map/ppermute | solution.py:354
  68.0 18.0 %collective-permute-start.28 = (bf16[2,512,128]{2,1,0:T(8,128)(2,1)S(1)}, bf16[2,512,128]{2,1,0:T(8,128)(2,1)S(1)}, u32[]{:S(2)}, u32[]{:S(2)}) collective-permute-start(bf16[2,512,128]{2,1,0:T(8,128)(2,1)S(1)} %get-tuple-element.78), channel_id=1, source_target_pairs={{0,32},{8,40},{16,48},{24,56},{32,0},{40,8},{48,16},{56,24},{64,96... | collective-permute-start | bytes 786440 | tf_op jit(solution)/shard_map/ppermute | solution.py:354
  71.6 20.3 %collective-permute-start.23 = (bf16[2,512,128]{2,1,0:T(8,128)(2,1)S(1)}, bf16[2,512,128]{2,1,0:T(8,128)(2,1)S(1)}, u32[]{:S(2)}, u32[]{:S(2)}) collective-permute-start(bf16[2,512,128]{2,1,0:T(8,128)(2,1)S(1)} %get-tuple-element.72), channel_id=1, source_target_pairs={{0,16},{8,24},{16,32},{24,40},{32,48},{40,56},{48,0},{56,8},{64,80... | collective-permute-start | bytes 786440 | tf_op jit(solution)/shard_map/ppermute | solution.py:354
  72.9 20.6 %collective-permute-start.24 = (bf16[2,512,128]{2,1,0:T(8,128)(2,1)S(1)}, bf16[2,512,128]{2,1,0:T(8,128)(2,1)S(1)}, u32[]{:S(2)}, u32[]{:S(2)}) collective-permute-start(bf16[2,512,128]{2,1,0:T(8,128)(2,1)S(1)} %get-tuple-element.73), channel_id=1, source_target_pairs={{0,48},{8,56},{16,0},{24,8},{32,16},{40,24},{48,32},{56,40},{64,11... | collective-permute-start | bytes 786440 | tf_op jit(solution)/shard_map/ppermute | solution.py:354
  76.7 20.1 %collective-permute-start.25 = (bf16[2,512,128]{2,1,0:T(8,128)(2,1)S(1)}, bf16[2,512,128]{2,1,0:T(8,128)(2,1)S(1)}, u32[]{:S(2)}, u32[]{:S(2)}) collective-permute-start(bf16[2,512,128]{2,1,0:T(8,128)(2,1)S(1)} %get-tuple-element.74), channel_id=1, source_target_pairs={{0,32},{8,40},{16,48},{24,56},{32,0},{40,8},{48,16},{56,24},{64,96... | collective-permute-start | bytes 786440 | tf_op jit(solution)/shard_map/ppermute | solution.py:354
  82.3 22.2 %collective-permute-start.21 = (bf16[5,160,128]{2,1,0:T(8,128)(2,1)S(1)}, bf16[5,160,128]{2,1,0:T(8,128)(2,1)S(1)}, u32[]{:S(2)}, u32[]{:S(2)}) collective-permute-start(bf16[5,160,128]{2,1,0:T(8,128)(2,1)S(1)} %shard_map.112), channel_id=1, source_target_pairs={{24,0},{32,8},{40,16},{48,24},{56,32},{64,40},{72,48},{80,56},{88,... | collective-permute-start | bytes 614408 | tf_op jit(solution)/shard_map/ppermute | solution.py:342
  86.0 18.4 %collective-permute-start.20 = (bf16[5,160,128]{2,1,0:T(8,128)(2,1)S(1)}, bf16[5,160,128]{2,1,0:T(8,128)(2,1)S(1)}, u32[]{:S(2)}, u32[]{:S(2)}) collective-permute-start(bf16[5,160,128]{2,1,0:T(8,128)(2,1)S(1)} %shard_map.112), channel_id=1, source_target_pairs={{8,0},{16,8},{24,16},{32,24},{40,32},{48,40},{56,48},{64,56},{72,6... | collective-permute-start | bytes 614408 | tf_op jit(solution)/shard_map/ppermute | solution.py:342
  97.8 9.9 %collective-permute-start.29 = (bf16[512,128]{1,0:T(8,128)(2,1)S(1)}, bf16[512,128]{1,0:T(8,128)(2,1)S(1)}, u32[]{:S(2)}, u32[]{:S(2)}) collective-permute-start(bf16[512,128]{1,0:T(8,128)(2,1)S(1)} %get-tuple-element.80), channel_id=1, source_target_pairs={{0,64},{8,72},{16,80},{24,88},{32,96},{40,104},{48,112},{56,120},{... | collective-permute-start | bytes 393224 | tf_op jit(solution)/shard_map/ppermute | solution.py:354
  102.9 5.9 %collective-permute-start.30 = (bf16[512,128]{1,0:T(8,128)(2,1)S(1)}, bf16[512,128]{1,0:T(8,128)(2,1)S(1)}, u32[]{:S(2)}, u32[]{:S(2)}) collective-permute-start(bf16[512,128]{1,0:T(8,128)(2,1)S(1)} %get-tuple-element.81), channel_id=1, source_target_pairs={{0,192},{8,200},{16,208},{24,216},{32,224},{40,232},{48,240},{56,2... | collective-permute-start | bytes 393224 | tf_op jit(solution)/shard_map/ppermute | solution.py:354
  102.9 7.8 %collective-permute-start.31 = (bf16[512,128]{1,0:T(8,128)(2,1)S(1)}, bf16[512,128]{1,0:T(8,128)(2,1)S(1)}, u32[]{:S(2)}, u32[]{:S(2)}) collective-permute-start(bf16[512,128]{1,0:T(8,128)(2,1)S(1)} %get-tuple-element.82), channel_id=1, source_target_pairs={{0,128},{8,136},{16,144},{24,152},{32,160},{40,168},{48,176},{56,1... | collective-permute-start | bytes 393224 | tf_op jit(solution)/shard_map/ppermute | solution.py:354
  (15 other events, 133.0 us)
where the time goes:
time: 112 us; the launch traced here: 111 us
  starting transfers between devices  50.4 us (45%)
  waiting for transfers between devices  26.9 us (24%)
  Pallas kernels  25.6 us (23%)
  local copies, waits for them, and re-layouts  7.69 us (7%)
    ppermute x12, starting transfers between devices, on_device(): pieces[-d * step] = [lax.ppermute(x, 'head', ring[d]) for x in before]  18.5 us
    ppermute x12, waiting for transfers between devices, on_device(): send = lambda x, pairs: lax.ppermute(x, 'ctx', pairs)  17.8 us
    ppermute x12, starting transfers between devices, on_device(): send = lambda x, pairs: lax.ppermute(x, 'ctx', pairs)  14.6 us
    ppermute x2, starting transfers between devices, exchange(): lax.ppermute(pair, 'ctx', shift(sign))  6.35 us
    unnamed x30, local copies, waits for them, and re-layouts  6.02 us
    ppermute x12, waiting for transfers between devices, on_device(): pieces[-d * step] = [lax.ppermute(x, 'head', ring[d]) for x in before]  5.14 us
    pallas_call x3, Pallas kernels, terms(): call(functools.partial(partial_terms, n), [block, block], 1 + 2 * n, n *...  4.3 us
    pallas_call x1, Pallas kernels, on_device(): call(local_grads, [((128, TOK), f32), ((TOK, TOK), f32)], 10, 2 ** 31, 4...  3.91 us
  transfers between devices with their start and end apart: 32, of which 13 were waited for; matrix products, arithmetic and copies ran while one was open for 1% of the time, Pallas kernels for 22%

commit v1 on v0

--- a/solution.py
+++ b/solution.py
@@ -373,7 +373,7 @@
             compiler_params=pltpu.CompilerParams(vmem_limit_bytes=LIMIT),
             cost_estimate=pl.CostEstimate(flops=2**20, bytes_accessed=2**21, transcendentals=0),
         )(ids, *[f[0] for f in found], *[f[1] for f in found])
-        return [parts[0]] + [send(parts[d], along(0, d)) for d in (1, 3, 2)]
+        return [parts[0]] + [send(parts[d], along(0, d)) for d in (2, 1, 3)]
 
     steps = [(0, 1, -2, -1), (2, 3, 4, -3)]
     early = spread((0, -2), [terms((0, 1, -2, -1))])
@@ -409,7 +409,7 @@
         compiler_params=pltpu.CompilerParams(vmem_limit_bytes=LIMIT),
         cost_estimate=pl.CostEstimate(flops=2**20, bytes_accessed=2**21, transcendentals=0),
     )(ids, *early, *rest)
-    across = [send(sums[d], along(d, 0)) for d in (1, 3, 2)]
+    across = [send(sums[d], along(d, 0)) for d in (2, 1, 3)]
     proj_grad = call(sum_along_y, [((TOK, HEAD), f32)], 4, 2**19, 2**20, False)(
         sums[0], *across
     )[0]

time: 112 us -> 108 us (0.964)
  waiting for transfers between devices: 26.9 us -> 22 us
    ppermute x12, waiting for transfers between devices: 17.8 us -> 8.26 us  [on_device(): send = lambda x, pairs: lax.ppermute(x, 'ctx', pairs)]
    ppermute x12, starting transfers between devices: 14.6 us -> 12.2 us  [on_device(): send = lambda x, pairs: lax.ppermute(x, 'ctx', pairs)]
    ppermute x2, waiting for transfers between devices: 1.13 us -> 3.52 us  [exchange(): lax.ppermute(pair, 'ctx', shift(3 * sign))]
    ppermute x2, waiting for transfers between devices: 0.01 us -> 2.21 us  [exchange(): got = lax.ppermute(mine, 'ctx', shift(sign))]
    ppermute x2, starting transfers between devices: 3.83 us -> 5.42 us  [exchange(): got = lax.ppermute(mine, 'ctx', shift(sign))]
    ppermute x2, starting transfers between devices: 3.83 us -> 5.4 us  [exchange(): lax.ppermute(pair, 'ctx', shift(3 * sign))]
  transfers between devices with their start and end apart: 32 -> 32, of which waited for: 13 -> 12; matrix products, arithmetic and copies ran while one was open for 1% -> 1% of each run, Pallas kernels for 22% -> 23%
where the time goes in v1:
time: 108 us; the launch traced here: 107 us
  starting transfers between devices  51.1 us (47%)
  Pallas kernels  25.6 us (24%)
  waiting for transfers between devices  22 us (20%)
  local copies, waits for them, and re-layouts  7.69 us (7%)
    ppermute x12, starting transfers between devices, on_device(): pieces[-d * step] = [lax.ppermute(x, 'head', ring[d]) for x in before]  18.5 us
    ppermute x12, starting transfers between devices, on_device(): send = lambda x, pairs: lax.ppermute(x, 'ctx', pairs)  12.2 us
    ppermute x12, waiting for transfers between devices, on_device(): send = lambda x, pairs: lax.ppermute(x, 'ctx', pairs)  8.26 us
    ppermute x2, starting transfers between devices, exchange(): lax.ppermute(pair, 'ctx', shift(sign))  6.35 us
    unnamed x30, local copies, waits for them, and re-layouts  6.02 us
    ppermute x2, starting transfers between devices, exchange(): got = lax.ppermute(mine, 'ctx', shift(sign))  5.42 us
    ppermute x2, starting transfers between devices, exchange(): lax.ppermute(pair, 'ctx', shift(3 * sign))  5.4 us
    ppermute x12, waiting for transfers between devices, on_device(): pieces[-d * step] = [lax.ppermute(x, 'head', ring[d]) for x in before]  5.14 us
  transfers between devices with their start and end apart: 32, of which 12 were waited for; matrix products, arithmetic and copies ran while one was open for 1% of the time, Pallas kernels for 23%

profile of v1, /device:TPU:14, one launch (start us, length us, event | category | flops | bytes accessed | tf_op | source)
XLA Modules:
  0.0 107.2 jit_solution(16417714272509756486)
XLA Ops:
  1.7 2.0 %collective-permute-start.2 = (bf16[256,512]{1,0:T(8,128)(2,1)S(1)}, bf16[256,512]{1,0:T(8,128)(2,1)S(1)}, u32[]{:S(2)}, u32[]{:S(2)}) collective-permute-start(bf16[256,512]{1,0:T(8,128)(2,1)S(1)} %get-tuple-element.44.refs_0_), channel_id=1, source_target_pairs={{0,1},{1,2},{2,3},{3,4},{4,5},{5,6},{6,7},{7,0},{8,9},{9,10},{10,1... | collective-permute-start | bytes 786440 | tf_op jit(solution)/shard_map/ppermute | solution.py:336
  4.3 3.1 %shard_map.103 = (bf16[5,160,128]{2,1,0:T(8,128)(2,1)}, bf16[128,512]{1,0:T(8,128)(2,1)}, f32[8,512]{1,0:T(8,128)}) custom-call(s32[6]{0:T(128)} %stack.27.ids, s32[1,128]{1,0:T(1,128)} %bitcast.7, bf16[512,128]{1,0:T(8,128)(2,1)} %qk, bf16[512,512]{1,0:T(8,128)(2,1)} %v.7, bf16[160,32]{1,0:T(8,128)(2,1)} %constant.63.clone.pick, f32[160,128]{1,0:T(8,128)} %constant.65.clone.cols), custom_call_target="tpu_custom_call" | custom-call | flops 134217728 | bytes 2097152 | tf_op jit(solution)/shard_map/pallas_call | solution.py:320
  7.4 4.0 %collective-permute-start.1 = (bf16[256,512]{1,0:T(8,128)(2,1)S(1)}, bf16[256,512]{1,0:T(8,128)(2,1)S(1)}, u32[]{:S(2)}, u32[]{:S(2)}) collective-permute-start(bf16[256,512]{1,0:T(8,128)(2,1)S(1)} %get-tuple-element.48.refs_1_), channel_id=1, source_target_pairs={{0,7},{1,0},{2,1},{3,2},{4,3},{5,4},{6,5},{7,6},{8,15},{9,8},{10,9... | collective-permute-start | bytes 786440 | tf_op jit(solution)/shard_map/ppermute | solution.py:336
  11.4 1.9 %collective-permute-start.14 = (bf16[5,160,128]{2,1,0:T(8,128)(2,1)}, bf16[5,160,128]{2,1,0:T(8,128)(2,1)S(1)}, u32[]{:S(2)}, u32[]{:S(2)}) collective-permute-start(bf16[5,160,128]{2,1,0:T(8,128)(2,1)} %get-tuple-element.51.own), channel_id=1, source_target_pairs={{0,8},{8,16},{16,24},{24,32},{32,40},{40,48},{48,56},{56,64},{64,7... | collective-permute-start | bytes 614408 | tf_op jit(solution)/shard_map/ppermute | solution.py:340
  13.3 2.0 %collective-permute-start = (bf16[256,512]{1,0:T(8,128)(2,1)S(1)}, bf16[256,512]{1,0:T(8,128)(2,1)S(1)}, u32[]{:S(2)}, u32[]{:S(2)}) collective-permute-start(bf16[256,512]{1,0:T(8,128)(2,1)S(1)} %get-tuple-element.44.refs_0_), channel_id=1, source_target_pairs={{0,7},{1,0},{2,1},{3,2},{4,3},{5,4},{6,5},{7,6},{8,15},{9,8},{10,9... | collective-permute-start | bytes 786440 | tf_op jit(solution)/shard_map/ppermute | solution.py:336
  15.5 1.5 %collective-permute-done.1.refs_3_ = bf16[256,512]{1,0:T(8,128)(2,1)S(1)} collective-permute-done((bf16[256,512]{1,0:T(8,128)(2,1)S(1)}, bf16[256,512]{1,0:T(8,128)(2,1)S(1)}, u32[]{:S(2)}, u32[]{:S(2)}) %collective-permute-start.1) | collective-permute-done | bytes 262176 | tf_op jit(solution)/shard_map/ppermute | solution.py:336
  17.0 3.7 %collective-permute-start.7 = (bf16[256,512]{1,0:T(8,128)(2,1)S(1)}, bf16[256,512]{1,0:T(8,128)(2,1)S(1)}, u32[]{:S(2)}, u32[]{:S(2)}) collective-permute-start(bf16[256,512]{1,0:T(8,128)(2,1)S(1)} %collective-permute-done.1.refs_3_), channel_id=1, source_target_pairs={{0,7},{1,0},{2,1},{3,2},{4,3},{5,4},{6,5},{7,6},{8,15},{9,8},{10,9... | collective-permute-start | bytes 786440 | tf_op jit(solution)/shard_map/ppermute | solution.py:336
  22.7 1.9 %collective-permute-start.16 = (bf16[5,160,128]{2,1,0:T(8,128)(2,1)S(1)}, bf16[5,160,128]{2,1,0:T(8,128)(2,1)S(1)}, u32[]{:S(2)}, u32[]{:S(2)}) collective-permute-start(bf16[5,160,128]{2,1,0:T(8,128)(2,1)S(1)} %shard_map.105), channel_id=1, source_target_pairs={{0,24},{8,32},{16,40},{24,48},{32,56},{40,64},{48,72},{56,80},{64,... | collective-permute-start | bytes 614408 | tf_op jit(solution)/shard_map/ppermute | solution.py:342
  24.6 4.4 %collective-permute-start.15 = (bf16[5,160,128]{2,1,0:T(8,128)(2,1)S(1)}, bf16[5,160,128]{2,1,0:T(8,128)(2,1)S(1)}, u32[]{:S(2)}, u32[]{:S(2)}) collective-permute-start(bf16[5,160,128]{2,1,0:T(8,128)(2,1)S(1)} %shard_map.105), channel_id=1, source_target_pairs={{0,8},{8,16},{16,24},{24,32},{32,40},{40,48},{48,56},{56,64},{64,7... | collective-permute-start | bytes 614408 | tf_op jit(solution)/shard_map/ppermute | solution.py:342
  32.2 2.4 %collective-permute-start.9 = (bf16[256,512]{1,0:T(8,128)(2,1)S(1)}, bf16[256,512]{1,0:T(8,128)(2,1)S(1)}, u32[]{:S(2)}, u32[]{:S(2)}) collective-permute-start(bf16[256,512]{1,0:T(8,128)(2,1)S(1)} %collective-permute-done.7.refs_9_.refs_1_), channel_id=1, source_target_pairs={{0,7},{1,0},{2,1},{3,2},{4,3},{5,4},{6,5},{7,6},{8,15},{9,8},{10,9... | collective-permute-start | bytes 786440 | tf_op jit(solution)/shard_map/ppermute | solution.py:336
  38.9 2.6 %shard_map.106 = (bf16[512,512]{1,0:T(8,128)(2,1)S(1)}, f32[512,512]{1,0:T(8,128)S(1)}, f32[8,512]{1,0:T(8,128)S(1)}) custom-call(bf16[128,512]{1,0:T(8,128)(2,1)S(1)} %copy-done.4, bf16[512,512]{1,0:T(8,128)(2,1)S(1)} %copy-done, f32[8,512]{1,0:T(8,128)S(1)} %copy-done.9, bf16[160,32]{1,0:T(8,128)(2,1)S(1)} %copy-done.6, f32[160,128]{1,0:T(8,128)S(1)} %copy-done.2, ...), custom_call_target="tpu_custom_call" | custom-call | flops 1073741824 | bytes 4194304 | tf_op jit(solution)/shard_map/pallas_call | solution.py:345
  41.6 2.2 %collective-permute-start.8 = (bf16[256,512]{1,0:T(8,128)(2,1)S(1)}, bf16[256,512]{1,0:T(8,128)(2,1)S(1)}, u32[]{:S(2)}, u32[]{:S(2)}) collective-permute-start(bf16[256,512]{1,0:T(8,128)(2,1)S(1)} %collective-permute-done.6.refs_8_.refs_0_), channel_id=1, source_target_pairs={{0,7},{1,0},{2,1},{3,2},{4,3},{5,4},{6,5},{7,6},{8,15},{9,8},{10,9... | collective-permute-start | bytes 786440 | tf_op jit(solution)/shard_map/ppermute | solution.py:336
  43.9 1.8 %collective-permute-done.10.refs_14_.refs_2_ = bf16[256,512]{1,0:T(8,128)(2,1)S(1)} collective-permute-done((bf16[256,512]{1,0:T(8,128)(2,1)S(1)}, bf16[256,512]{1,0:T(8,128)(2,1)S(1)}, u32[]{:S(2)}, u32[]{:S(2)}) %collective-permute-start.10) | collective-permute-done | bytes 262176 | tf_op jit(solution)/shard_map/ppermute | solution.py:336
  45.8 3.1 %collective-permute-start.12 = (bf16[256,512]{1,0:T(8,128)(2,1)S(1)}, bf16[256,512]{1,0:T(8,128)(2,1)S(1)}, u32[]{:S(2)}, u32[]{:S(2)}) collective-permute-start(bf16[256,512]{1,0:T(8,128)(2,1)S(1)} %collective-permute-done.9.refs_11_.refs_3_), channel_id=1, source_target_pairs={{0,7},{1,0},{2,1},{3,2},{4,3},{5,4},{6,5},{7,6},{8,15},{9,8},{10,9... | collective-permute-start | bytes 786440 | tf_op jit(solution)/shard_map/ppermute | solution.py:337
  48.9 1.8 %shard_map.114 = (bf16[8,512,128]{2,1,0:T(8,128)(2,1)S(1)}, bf16[8,512,128]{2,1,0:T(8,128)(2,1)S(1)}) custom-call(s32[6]{0:T(128)S(1)} %copy-done.13, bf16[512,512]{1,0:T(8,128)(2,1)S(1)} %get-tuple-element.57.att, bf16[256,512]{1,0:T(8,128)(2,1)S(1)} %get-tuple-element.44.refs_0_, bf16[256,512]{1,0:T(8,128)(2,1)S(1)} %get-tuple-element.48.refs_1_, ...), custom_call_target="tpu_custom_call" | custom-call | flops 1073741824 | bytes 4194304 | tf_op jit(solution)/shard_map/pallas_call | solution.py:359
  52.7 1.6 %collective-permute-done.13.refs_15_.refs_3_ = bf16[256,512]{1,0:T(8,128)(2,1)S(1)} collective-permute-done((bf16[256,512]{1,0:T(8,128)(2,1)S(1)}, bf16[256,512]{1,0:T(8,128)(2,1)S(1)}, u32[]{:S(2)}, u32[]{:S(2)}) %collective-permute-start.13) | collective-permute-done | bytes 262176 | tf_op jit(solution)/shard_map/ppermute | solution.py:336
  54.2 2.8 %collective-permute-done.11.refs_12_.refs_0_ = bf16[256,512]{1,0:T(8,128)(2,1)S(1)} collective-permute-done((bf16[256,512]{1,0:T(8,128)(2,1)S(1)}, bf16[256,512]{1,0:T(8,128)(2,1)S(1)}, u32[]{:S(2)}, u32[]{:S(2)}) %collective-permute-start.11) | collective-permute-done | bytes 262176 | tf_op jit(solution)/shard_map/ppermute | solution.py:337
  58.5 2.9 %shard_map.104.up = f32[512,512]{1,0:T(8,128)S(1)} custom-call(s32[6]{0:T(128)S(1)} %copy-done.13, bf16[512,4096]{1,0:T(8,128)(2,1)S(1)} %copy-done.14, bf16[256,512]{1,0:T(8,128)(2,1)S(1)} %get-tuple-element.44.refs_0_, bf16[256,512]{1,0:T(8,128)(2,1)S(1)} %get-tuple-element.48.refs_1_, bf16[256,512]{1,0:T(8,128)(2,1)S(1)} %collective-permute-done.refs_2_, ...), custom_call_target="tpu_custom_call" | custom-call | flops 4294967296 | bytes 9437184 | tf_op jit(solution)/shard_map/pallas_call | solution.py:383
  64.5 3.5 %collective-permute-start.19 = (bf16[5,160,128]{2,1,0:T(8,128)(2,1)S(1)}, bf16[5,160,128]{2,1,0:T(8,128)(2,1)S(1)}, u32[]{:S(2)}, u32[]{:S(2)}) collective-permute-start(bf16[5,160,128]{2,1,0:T(8,128)(2,1)S(1)} %get-tuple-element.60.own), channel_id=1, source_target_pairs={{8,0},{16,8},{24,16},{32,24},{40,32},{48,40},{56,48},{64,56},{72,6... | collective-permute-start | bytes 614408 | tf_op jit(solution)/shard_map/ppermute | solution.py:340
  71.1 2.3 %collective-permute-start.23 = (bf16[2,512,128]{2,1,0:T(8,128)(2,1)S(1)}, bf16[2,512,128]{2,1,0:T(8,128)(2,1)S(1)}, u32[]{:S(2)}, u32[]{:S(2)}) collective-permute-start(bf16[2,512,128]{2,1,0:T(8,128)(2,1)S(1)} %get-tuple-element.72), channel_id=1, source_target_pairs={{0,32},{8,40},{16,48},{24,56},{32,0},{40,8},{48,16},{56,24},{64,96... | collective-permute-start | bytes 786440 | tf_op jit(solution)/shard_map/ppermute | solution.py:354
  73.4 2.2 %collective-permute-done.19.got = bf16[5,160,128]{2,1,0:T(8,128)(2,1)S(1)} collective-permute-done((bf16[5,160,128]{2,1,0:T(8,128)(2,1)S(1)}, bf16[5,160,128]{2,1,0:T(8,128)(2,1)S(1)}, u32[]{:S(2)}, u32[]{:S(2)}) %collective-permute-start.19) | collective-permute-done | bytes 204832 | tf_op jit(solution)/shard_map/ppermute | solution.py:340
  75.6 2.1 %collective-permute-start.24 = (bf16[2,512,128]{2,1,0:T(8,128)(2,1)S(1)}, bf16[2,512,128]{2,1,0:T(8,128)(2,1)S(1)}, u32[]{:S(2)}, u32[]{:S(2)}) collective-permute-start(bf16[2,512,128]{2,1,0:T(8,128)(2,1)S(1)} %get-tuple-element.73), channel_id=1, source_target_pairs={{0,16},{8,24},{16,32},{24,40},{32,48},{40,56},{48,0},{56,8},{64,80... | collective-permute-start | bytes 786440 | tf_op jit(solution)/shard_map/ppermute | solution.py:354
  79.1 3.5 %collective-permute-start.21 = (bf16[5,160,128]{2,1,0:T(8,128)(2,1)S(1)}, bf16[5,160,128]{2,1,0:T(8,128)(2,1)S(1)}, u32[]{:S(2)}, u32[]{:S(2)}) collective-permute-start(bf16[5,160,128]{2,1,0:T(8,128)(2,1)S(1)} %shard_map.112), channel_id=1, source_target_pairs={{24,0},{32,8},{40,16},{48,24},{56,32},{64,40},{72,48},{80,56},{88,... | collective-permute-start | bytes 614408 | tf_op jit(solution)/shard_map/ppermute | solution.py:342
  82.6 3.0 %collective-permute-done.28.refs_7_ = bf16[2,512,128]{2,1,0:T(8,128)(2,1)S(1)} collective-permute-done((bf16[2,512,128]{2,1,0:T(8,128)(2,1)S(1)}, bf16[2,512,128]{2,1,0:T(8,128)(2,1)S(1)}, u32[]{:S(2)}, u32[]{:S(2)}) %collective-permute-start.28) | collective-permute-done | bytes 262176 | tf_op jit(solution)/shard_map/ppermute | solution.py:354
  85.6 1.9 %collective-permute-start.20 = (bf16[5,160,128]{2,1,0:T(8,128)(2,1)S(1)}, bf16[5,160,128]{2,1,0:T(8,128)(2,1)S(1)}, u32[]{:S(2)}, u32[]{:S(2)}) collective-permute-start(bf16[5,160,128]{2,1,0:T(8,128)(2,1)S(1)} %shard_map.112), channel_id=1, source_target_pairs={{8,0},{16,8},{24,16},{32,24},{40,32},{48,40},{56,48},{64,56},{72,6... | collective-permute-start | bytes 614408 | tf_op jit(solution)/shard_map/ppermute | solution.py:342
  87.5 3.9 %shard_map.108 = (f32[128,512]{1,0:T(8,128)S(1)}, f32[512,512]{1,0:T(8,128)S(1)}) custom-call(bf16[512,512]{1,0:T(8,128)(2,1)S(1)} %get-tuple-element.54.ng, f32[8,512]{1,0:T(8,128)S(1)} %get-tuple-element.55.dg, bf16[128,512]{1,0:T(8,128)(2,1)S(1)} %copy-done.5, bf16[512,512]{1,0:T(8,128)(2,1)S(1)} %copy-done.1, f32[8,512]{1,0:T(8,128)S(1)} %copy-done.10, ...), custom_call_target="tpu_custom_call" | custom-call | flops 2147483648 | bytes 4194304 | tf_op jit(solution)/shard_map/pallas_call | solution.py:398
  91.5 1.9 %collective-permute-done.25.refs_3_ = bf16[2,512,128]{2,1,0:T(8,128)(2,1)S(1)} collective-permute-done((bf16[2,512,128]{2,1,0:T(8,128)(2,1)S(1)}, bf16[2,512,128]{2,1,0:T(8,128)(2,1)S(1)}, u32[]{:S(2)}, u32[]{:S(2)}) %collective-permute-start.25) | collective-permute-done | bytes 262176 | tf_op jit(solution)/shard_map/ppermute | solution.py:354
  94.3 1.6 %collective-permute-start.29 = (bf16[512,128]{1,0:T(8,128)(2,1)S(1)}, bf16[512,128]{1,0:T(8,128)(2,1)S(1)}, u32[]{:S(2)}, u32[]{:S(2)}) collective-permute-start(bf16[512,128]{1,0:T(8,128)(2,1)S(1)} %get-tuple-element.80), channel_id=1, source_target_pairs={{0,128},{8,136},{16,144},{24,152},{32,160},{40,168},{48,176},{56,1... | collective-permute-start | bytes 393224 | tf_op jit(solution)/shard_map/ppermute | solution.py:354
  96.5 2.0 %collective-permute-start.31 = (bf16[512,128]{1,0:T(8,128)(2,1)S(1)}, bf16[512,128]{1,0:T(8,128)(2,1)S(1)}, u32[]{:S(2)}, u32[]{:S(2)}) collective-permute-start(bf16[512,128]{1,0:T(8,128)(2,1)S(1)} %get-tuple-element.82), channel_id=1, source_target_pairs={{0,192},{8,200},{16,208},{24,216},{32,224},{40,232},{48,240},{56,2... | collective-permute-start | bytes 393224 | tf_op jit(solution)/shard_map/ppermute | solution.py:354
  98.5 2.4 %collective-permute-done.21.far = bf16[5,160,128]{2,1,0:T(8,128)(2,1)S(1)} collective-permute-done((bf16[5,160,128]{2,1,0:T(8,128)(2,1)S(1)}, bf16[5,160,128]{2,1,0:T(8,128)(2,1)S(1)}, u32[]{:S(2)}, u32[]{:S(2)}) %collective-permute-start.21) | collective-permute-done | bytes 204832 | tf_op jit(solution)/shard_map/ppermute | solution.py:342
  100.9 3.2 %shard_map.113 = (bf16[512,128]{1,0:T(8,128)(2,1)}, bf16[512,512]{1,0:T(8,128)(2,1)}) custom-call(f32[128,512]{1,0:T(8,128)S(1)} %get-tuple-element.56.qkg, f32[512,512]{1,0:T(8,128)S(1)} %get-tuple-element.66.vg, bf16[128,512]{1,0:T(8,128)(2,1)S(1)} %copy-done.5, bf16[512,512]{1,0:T(8,128)(2,1)S(1)} %copy-done.1, f32[8,512]{1,0:T(8,128)S(1)} %copy-done.10, ...), custom_call_target="tpu_custom_call" | custom-call | flops 536870912 | bytes 4194304 | tf_op jit(solution)/shard_map/pallas_call | solution.py:416
  104.2 2.3 %collective-permute-done.31.c = bf16[512,128]{1,0:T(8,128)(2,1)S(1)} collective-permute-done((bf16[512,128]{1,0:T(8,128)(2,1)S(1)}, bf16[512,128]{1,0:T(8,128)(2,1)S(1)}, u32[]{:S(2)}, u32[]{:S(2)}) %collective-permute-start.31) | collective-permute-done | bytes 131104 | tf_op jit(solution)/shard_map/ppermute | solution.py:354
  (79 shorter events, 24.5 us)
Async XLA Ops:
  1.7 13.7 %collective-permute-start.2 = (bf16[256,512]{1,0:T(8,128)(2,1)S(1)}, bf16[256,512]{1,0:T(8,128)(2,1)S(1)}, u32[]{:S(2)}, u32[]{:S(2)}) collective-permute-start(bf16[256,512]{1,0:T(8,128)(2,1)S(1)} %get-tuple-element.44.refs_0_), channel_id=1, source_target_pairs={{0,1},{1,2},{2,3},{3,4},{4,5},{5,6},{6,7},{7,0},{8,9},{9,10},{10,1... | collective-permute-start | bytes 786440 | tf_op jit(solution)/shard_map/ppermute | solution.py:336
  7.4 9.6 %collective-permute-start.1 = (bf16[256,512]{1,0:T(8,128)(2,1)S(1)}, bf16[256,512]{1,0:T(8,128)(2,1)S(1)}, u32[]{:S(2)}, u32[]{:S(2)}) collective-permute-start(bf16[256,512]{1,0:T(8,128)(2,1)S(1)} %get-tuple-element.48.refs_1_), channel_id=1, source_target_pairs={{0,7},{1,0},{2,1},{3,2},{4,3},{5,4},{6,5},{7,6},{8,15},{9,8},{10,9... | collective-permute-start | bytes 786440 | tf_op jit(solution)/shard_map/ppermute | solution.py:336
  11.4 9.3 %collective-permute-start.14 = (bf16[5,160,128]{2,1,0:T(8,128)(2,1)}, bf16[5,160,128]{2,1,0:T(8,128)(2,1)S(1)}, u32[]{:S(2)}, u32[]{:S(2)}) collective-permute-start(bf16[5,160,128]{2,1,0:T(8,128)(2,1)} %get-tuple-element.51.own), channel_id=1, source_target_pairs={{0,8},{8,16},{16,24},{24,32},{32,40},{40,48},{48,56},{56,64},{64,7... | collective-permute-start | bytes 614408 | tf_op jit(solution)/shard_map/ppermute | solution.py:340
  13.3 11.3 %collective-permute-start = (bf16[256,512]{1,0:T(8,128)(2,1)S(1)}, bf16[256,512]{1,0:T(8,128)(2,1)S(1)}, u32[]{:S(2)}, u32[]{:S(2)}) collective-permute-start(bf16[256,512]{1,0:T(8,128)(2,1)S(1)} %get-tuple-element.44.refs_0_), channel_id=1, source_target_pairs={{0,7},{1,0},{2,1},{3,2},{4,3},{5,4},{6,5},{7,6},{8,15},{9,8},{10,9... | collective-permute-start | bytes 786440 | tf_op jit(solution)/shard_map/ppermute | solution.py:336
  15.4 13.7 %collective-permute-start.4 = (bf16[256,512]{1,0:T(8,128)(2,1)S(1)}, bf16[256,512]{1,0:T(8,128)(2,1)S(1)}, u32[]{:S(2)}, u32[]{:S(2)}) collective-permute-start(bf16[256,512]{1,0:T(8,128)(2,1)S(1)} %get-tuple-element.48.refs_1_), channel_id=1, source_target_pairs={{0,1},{1,2},{2,3},{3,4},{4,5},{5,6},{6,7},{7,0},{8,9},{9,10},{10,1... | collective-permute-start | bytes 786440 | tf_op jit(solution)/shard_map/ppermute | solution.py:336
  15.4 15.9 %collective-permute-start.3 = (bf16[256,512]{1,0:T(8,128)(2,1)S(1)}, bf16[256,512]{1,0:T(8,128)(2,1)S(1)}, u32[]{:S(2)}, u32[]{:S(2)}) collective-permute-start(bf16[256,512]{1,0:T(8,128)(2,1)S(1)} %collective-permute-done.2.refs_6_), channel_id=1, source_target_pairs={{0,1},{1,2},{2,3},{3,4},{4,5},{5,6},{6,7},{7,0},{8,9},{9,10},{10,1... | collective-permute-start | bytes 786440 | tf_op jit(solution)/shard_map/ppermute | solution.py:336
  17.0 15.2 %collective-permute-start.7 = (bf16[256,512]{1,0:T(8,128)(2,1)S(1)}, bf16[256,512]{1,0:T(8,128)(2,1)S(1)}, u32[]{:S(2)}, u32[]{:S(2)}) collective-permute-start(bf16[256,512]{1,0:T(8,128)(2,1)S(1)} %collective-permute-done.1.refs_3_), channel_id=1, source_target_pairs={{0,7},{1,0},{2,1},{3,2},{4,3},{5,4},{6,5},{7,6},{8,15},{9,8},{10,9... | collective-permute-start | bytes 786440 | tf_op jit(solution)/shard_map/ppermute | solution.py:336
  22.7 8.6 %collective-permute-start.16 = (bf16[5,160,128]{2,1,0:T(8,128)(2,1)S(1)}, bf16[5,160,128]{2,1,0:T(8,128)(2,1)S(1)}, u32[]{:S(2)}, u32[]{:S(2)}) collective-permute-start(bf16[5,160,128]{2,1,0:T(8,128)(2,1)S(1)} %shard_map.105), channel_id=1, source_target_pairs={{0,24},{8,32},{16,40},{24,48},{32,56},{40,64},{48,72},{56,80},{64,... | collective-permute-start | bytes 614408 | tf_op jit(solution)/shard_map/ppermute | solution.py:342
  24.6 10.0 %collective-permute-start.15 = (bf16[5,160,128]{2,1,0:T(8,128)(2,1)S(1)}, bf16[5,160,128]{2,1,0:T(8,128)(2,1)S(1)}, u32[]{:S(2)}, u32[]{:S(2)}) collective-permute-start(bf16[5,160,128]{2,1,0:T(8,128)(2,1)S(1)} %shard_map.105), channel_id=1, source_target_pairs={{0,8},{8,16},{16,24},{24,32},{32,40},{40,48},{48,56},{56,64},{64,7... | collective-permute-start | bytes 614408 | tf_op jit(solution)/shard_map/ppermute | solution.py:342
  29.1 12.5 %collective-permute-start.6 = (bf16[256,512]{1,0:T(8,128)(2,1)S(1)}, bf16[256,512]{1,0:T(8,128)(2,1)S(1)}, u32[]{:S(2)}, u32[]{:S(2)}) collective-permute-start(bf16[256,512]{1,0:T(8,128)(2,1)S(1)} %collective-permute-done.refs_2_), channel_id=1, source_target_pairs={{0,7},{1,0},{2,1},{3,2},{4,3},{5,4},{6,5},{7,6},{8,15},{9,8},{10,9... | collective-permute-start | bytes 786440 | tf_op jit(solution)/shard_map/ppermute | solution.py:336
  31.3 12.5 %collective-permute-start.5 = (bf16[256,512]{1,0:T(8,128)(2,1)S(1)}, bf16[256,512]{1,0:T(8,128)(2,1)S(1)}, u32[]{:S(2)}, u32[]{:S(2)}) collective-permute-start(bf16[256,512]{1,0:T(8,128)(2,1)S(1)} %collective-permute-done.4.refs_7_), channel_id=1, source_target_pairs={{0,1},{1,2},{2,3},{3,4},{4,5},{5,6},{6,7},{7,0},{8,9},{9,10},{10,1... | collective-permute-start | bytes 786440 | tf_op jit(solution)/shard_map/ppermute | solution.py:336
  31.3 14.4 %collective-permute-start.10 = (bf16[256,512]{1,0:T(8,128)(2,1)S(1)}, bf16[256,512]{1,0:T(8,128)(2,1)S(1)}, u32[]{:S(2)}, u32[]{:S(2)}) collective-permute-start(bf16[256,512]{1,0:T(8,128)(2,1)S(1)} %collective-permute-done.3.refs_4_), channel_id=1, source_target_pairs={{0,1},{1,2},{2,3},{3,4},{4,5},{5,6},{6,7},{7,0},{8,9},{9,10},{10,1... | collective-permute-start | bytes 786440 | tf_op jit(solution)/shard_map/ppermute | solution.py:336
  32.2 13.6 %collective-permute-start.9 = (bf16[256,512]{1,0:T(8,128)(2,1)S(1)}, bf16[256,512]{1,0:T(8,128)(2,1)S(1)}, u32[]{:S(2)}, u32[]{:S(2)}) collective-permute-start(bf16[256,512]{1,0:T(8,128)(2,1)S(1)} %collective-permute-done.7.refs_9_.refs_1_), channel_id=1, source_target_pairs={{0,7},{1,0},{2,1},{3,2},{4,3},{5,4},{6,5},{7,6},{8,15},{9,8},{10,9... | collective-permute-start | bytes 786440 | tf_op jit(solution)/shard_map/ppermute | solution.py:336
  41.6 9.5 %collective-permute-start.8 = (bf16[256,512]{1,0:T(8,128)(2,1)S(1)}, bf16[256,512]{1,0:T(8,128)(2,1)S(1)}, u32[]{:S(2)}, u32[]{:S(2)}) collective-permute-start(bf16[256,512]{1,0:T(8,128)(2,1)S(1)} %collective-permute-done.6.refs_8_.refs_0_), channel_id=1, source_target_pairs={{0,7},{1,0},{2,1},{3,2},{4,3},{5,4},{6,5},{7,6},{8,15},{9,8},{10,9... | collective-permute-start | bytes 786440 | tf_op jit(solution)/shard_map/ppermute | solution.py:336
  43.8 10.5 %collective-permute-start.13 = (bf16[256,512]{1,0:T(8,128)(2,1)S(1)}, bf16[256,512]{1,0:T(8,128)(2,1)S(1)}, u32[]{:S(2)}, u32[]{:S(2)}) collective-permute-start(bf16[256,512]{1,0:T(8,128)(2,1)S(1)} %collective-permute-done.5.refs_5_), channel_id=1, source_target_pairs={{0,1},{1,2},{2,3},{3,4},{4,5},{5,6},{6,7},{7,0},{8,9},{9,10},{10,1... | collective-permute-start | bytes 786440 | tf_op jit(solution)/shard_map/ppermute | solution.py:336
  45.7 11.4 %collective-permute-start.11 = (bf16[256,512]{1,0:T(8,128)(2,1)S(1)}, bf16[256,512]{1,0:T(8,128)(2,1)S(1)}, u32[]{:S(2)}, u32[]{:S(2)}) collective-permute-start(bf16[256,512]{1,0:T(8,128)(2,1)S(1)} %collective-permute-done.10.refs_14_.refs_2_), channel_id=1, source_target_pairs={{0,1},{1,2},{2,3},{3,4},{4,5},{5,6},{6,7},{7,0},{8,9},{9,10},{10,1... | collective-permute-start | bytes 786440 | tf_op jit(solution)/shard_map/ppermute | solution.py:337
  45.8 11.3 %collective-permute-start.12 = (bf16[256,512]{1,0:T(8,128)(2,1)S(1)}, bf16[256,512]{1,0:T(8,128)(2,1)S(1)}, u32[]{:S(2)}, u32[]{:S(2)}) collective-permute-start(bf16[256,512]{1,0:T(8,128)(2,1)S(1)} %collective-permute-done.9.refs_11_.refs_3_), channel_id=1, source_target_pairs={{0,7},{1,0},{2,1},{3,2},{4,3},{5,4},{6,5},{7,6},{8,15},{9,8},{10,9... | collective-permute-start | bytes 786440 | tf_op jit(solution)/shard_map/ppermute | solution.py:337
  50.7 19.4 %collective-permute-start.22 = (bf16[8,512,128]{2,1,0:T(8,128)(2,1)S(1)}, bf16[8,512,128]{2,1,0:T(8,128)(2,1)S(1)}, u32[]{:S(2)}, u32[]{:S(2)}) collective-permute-start(bf16[8,512,128]{2,1,0:T(8,128)(2,1)S(1)} %get-tuple-element.70), channel_id=1, source_target_pairs={{0,8},{8,0},{16,24},{24,16},{32,40},{40,32},{48,56},{56,48},{64,72... | collective-permute-start | bytes 3145736 | tf_op jit(solution)/shard_map/ppermute | solution.py:354
  52.3 10.3 %collective-permute-start.17 = (bf16[4,512,128]{2,1,0:T(8,128)(2,1)S(1)}, bf16[4,512,128]{2,1,0:T(8,128)(2,1)S(1)}, u32[]{:S(2)}, u32[]{:S(2)}) collective-permute-start(bf16[4,512,128]{2,1,0:T(8,128)(2,1)S(1)} %get-tuple-element.62), channel_id=1, source_target_pairs={{0,8},{8,0},{16,24},{24,16},{32,40},{40,32},{48,56},{56,48},{64,72... | collective-permute-start | bytes 1572872 | tf_op jit(solution)/shard_map/ppermute | solution.py:354
  58.4 4.2 %collective-permute-start.18 = (bf16[4,512,128]{2,1,0:T(8,128)(2,1)S(1)}, bf16[4,512,128]{2,1,0:T(8,128)(2,1)S(1)}, u32[]{:S(2)}, u32[]{:S(2)}) collective-permute-start(bf16[4,512,128]{2,1,0:T(8,128)(2,1)S(1)} %get-tuple-element.63), channel_id=1, source_target_pairs={{0,8},{8,0},{16,24},{24,16},{32,40},{40,32},{48,56},{56,48},{64,72... | collective-permute-start | bytes 1572872 | tf_op jit(solution)/shard_map/ppermute | solution.py:354
  63.6 14.1 %collective-permute-start.26 = (bf16[2,512,128]{2,1,0:T(8,128)(2,1)S(1)}, bf16[2,512,128]{2,1,0:T(8,128)(2,1)S(1)}, u32[]{:S(2)}, u32[]{:S(2)}) collective-permute-start(bf16[2,512,128]{2,1,0:T(8,128)(2,1)S(1)} %get-tuple-element.76), channel_id=1, source_target_pairs={{0,32},{8,40},{16,48},{24,56},{32,0},{40,8},{48,16},{56,24},{64,96... | collective-permute-start | bytes 786440 | tf_op jit(solution)/shard_map/ppermute | solution.py:354
  64.5 11.1 %collective-permute-start.19 = (bf16[5,160,128]{2,1,0:T(8,128)(2,1)S(1)}, bf16[5,160,128]{2,1,0:T(8,128)(2,1)S(1)}, u32[]{:S(2)}, u32[]{:S(2)}) collective-permute-start(bf16[5,160,128]{2,1,0:T(8,128)(2,1)S(1)} %get-tuple-element.60.own), channel_id=1, source_target_pairs={{8,0},{16,8},{24,16},{32,24},{40,32},{48,40},{56,48},{64,56},{72,6... | collective-permute-start | bytes 614408 | tf_op jit(solution)/shard_map/ppermute | solution.py:340
  68.0 11.0 %collective-permute-start.27 = (bf16[2,512,128]{2,1,0:T(8,128)(2,1)S(1)}, bf16[2,512,128]{2,1,0:T(8,128)(2,1)S(1)}, u32[]{:S(2)}, u32[]{:S(2)}) collective-permute-start(bf16[2,512,128]{2,1,0:T(8,128)(2,1)S(1)} %get-tuple-element.77), channel_id=1, source_target_pairs={{0,16},{8,24},{16,32},{24,40},{32,48},{40,56},{48,0},{56,8},{64,80... | collective-permute-start | bytes 786440 | tf_op jit(solution)/shard_map/ppermute | solution.py:354
  69.1 16.5 %collective-permute-start.28 = (bf16[2,512,128]{2,1,0:T(8,128)(2,1)S(1)}, bf16[2,512,128]{2,1,0:T(8,128)(2,1)S(1)}, u32[]{:S(2)}, u32[]{:S(2)}) collective-permute-start(bf16[2,512,128]{2,1,0:T(8,128)(2,1)S(1)} %get-tuple-element.78), channel_id=1, source_target_pairs={{0,48},{8,56},{16,0},{24,8},{32,16},{40,24},{48,32},{56,40},{64,11... | collective-permute-start | bytes 786440 | tf_op jit(solution)/shard_map/ppermute | solution.py:354
  71.1 20.4 %collective-permute-start.23 = (bf16[2,512,128]{2,1,0:T(8,128)(2,1)S(1)}, bf16[2,512,128]{2,1,0:T(8,128)(2,1)S(1)}, u32[]{:S(2)}, u32[]{:S(2)}) collective-permute-start(bf16[2,512,128]{2,1,0:T(8,128)(2,1)S(1)} %get-tuple-element.72), channel_id=1, source_target_pairs={{0,32},{8,40},{16,48},{24,56},{32,0},{40,8},{48,16},{56,24},{64,96... | collective-permute-start | bytes 786440 | tf_op jit(solution)/shard_map/ppermute | solution.py:354
  75.6 15.9 %collective-permute-start.24 = (bf16[2,512,128]{2,1,0:T(8,128)(2,1)S(1)}, bf16[2,512,128]{2,1,0:T(8,128)(2,1)S(1)}, u32[]{:S(2)}, u32[]{:S(2)}) collective-permute-start(bf16[2,512,128]{2,1,0:T(8,128)(2,1)S(1)} %get-tuple-element.73), channel_id=1, source_target_pairs={{0,16},{8,24},{16,32},{24,40},{32,48},{40,56},{48,0},{56,8},{64,80... | collective-permute-start | bytes 786440 | tf_op jit(solution)/shard_map/ppermute | solution.py:354
  77.7 15.7 %collective-permute-start.25 = (bf16[2,512,128]{2,1,0:T(8,128)(2,1)S(1)}, bf16[2,512,128]{2,1,0:T(8,128)(2,1)S(1)}, u32[]{:S(2)}, u32[]{:S(2)}) collective-permute-start(bf16[2,512,128]{2,1,0:T(8,128)(2,1)S(1)} %get-tuple-element.74), channel_id=1, source_target_pairs={{0,48},{8,56},{16,0},{24,8},{32,16},{40,24},{48,32},{56,40},{64,11... | collective-permute-start | bytes 786440 | tf_op jit(solution)/shard_map/ppermute | solution.py:354
  79.1 21.9 %collective-permute-start.21 = (bf16[5,160,128]{2,1,0:T(8,128)(2,1)S(1)}, bf16[5,160,128]{2,1,0:T(8,128)(2,1)S(1)}, u32[]{:S(2)}, u32[]{:S(2)}) collective-permute-start(bf16[5,160,128]{2,1,0:T(8,128)(2,1)S(1)} %shard_map.112), channel_id=1, source_target_pairs={{24,0},{32,8},{40,16},{48,24},{56,32},{64,40},{72,48},{80,56},{88,... | collective-permute-start | bytes 614408 | tf_op jit(solution)/shard_map/ppermute | solution.py:342
  85.6 15.3 %collective-permute-start.20 = (bf16[5,160,128]{2,1,0:T(8,128)(2,1)S(1)}, bf16[5,160,128]{2,1,0:T(8,128)(2,1)S(1)}, u32[]{:S(2)}, u32[]{:S(2)}) collective-permute-start(bf16[5,160,128]{2,1,0:T(8,128)(2,1)S(1)} %shard_map.112), channel_id=1, source_target_pairs={{8,0},{16,8},{24,16},{32,24},{40,32},{48,40},{56,48},{64,56},{72,6... | collective-permute-start | bytes 614408 | tf_op jit(solution)/shard_map/ppermute | solution.py:342
  94.3 9.8 %collective-permute-start.29 = (bf16[512,128]{1,0:T(8,128)(2,1)S(1)}, bf16[512,128]{1,0:T(8,128)(2,1)S(1)}, u32[]{:S(2)}, u32[]{:S(2)}) collective-permute-start(bf16[512,128]{1,0:T(8,128)(2,1)S(1)} %get-tuple-element.80), channel_id=1, source_target_pairs={{0,128},{8,136},{16,144},{24,152},{32,160},{40,168},{48,176},{56,1... | collective-permute-start | bytes 393224 | tf_op jit(solution)/shard_map/ppermute | solution.py:354
  95.9 8.2 %collective-permute-start.30 = (bf16[512,128]{1,0:T(8,128)(2,1)S(1)}, bf16[512,128]{1,0:T(8,128)(2,1)S(1)}, u32[]{:S(2)}, u32[]{:S(2)}) collective-permute-start(bf16[512,128]{1,0:T(8,128)(2,1)S(1)} %get-tuple-element.81), channel_id=1, source_target_pairs={{0,64},{8,72},{16,80},{24,88},{32,96},{40,104},{48,112},{56,120},{... | collective-permute-start | bytes 393224 | tf_op jit(solution)/shard_map/ppermute | solution.py:354
  96.5 9.9 %collective-permute-start.31 = (bf16[512,128]{1,0:T(8,128)(2,1)S(1)}, bf16[512,128]{1,0:T(8,128)(2,1)S(1)}, u32[]{:S(2)}, u32[]{:S(2)}) collective-permute-start(bf16[512,128]{1,0:T(8,128)(2,1)S(1)} %get-tuple-element.82), channel_id=1, source_target_pairs={{0,192},{8,200},{16,208},{24,216},{32,224},{40,232},{48,240},{56,2... | collective-permute-start | bytes 393224 | tf_op jit(solution)/shard_map/ppermute | solution.py:354
  (15 other events, 132.2 us)
